TPU v7x, 32 devices: a whole 2x2x4 slice. The times are simulated.
32 devices in a mesh: replica: 8 (over z, x), tensor: 4 (over y, core).
Axes of the slice: x: 2, y: 2, z: 4, core: 2. Of those that a mesh axis runs over, the one named last changes fastest.
Arguments:
- tokens: bfloat16 [96, 1536], P(('replica', 'tensor')), may hold values from -6 to 6
- attn_gain: float32 [1536], replicated, may hold values from 0.5 to 1.5
- qkv_weight: bfloat16 [1536, 2560], P(None, 'tensor'), may hold values from -0.15625 to 0.15625
- out_weight: bfloat16 [1536, 1536], P('tensor'), may hold values from -0.15625 to 0.15625
- moe_gain: float32 [1536], replicated, may hold values from 0.5 to 1.5
- router: bfloat16 [1536, 8], replicated, may hold values from -0.15625 to 0.15625
- expert_gate_up: bfloat16 [1536, 2, 4096], P(None, None, 'tensor'), may hold values from -0.15625 to 0.15625
- expert_down: bfloat16 [4096, 1536], P('tensor'), may hold values from -0.25 to 0.25
- kv_cache: bfloat16 [192, 2, 128, 512], P(('replica', 'tensor')), may hold values from -240 to 240
- page_table: int32 [64, 2], P('replica'), may hold values from 0 to 21, as said below
- home_len: int32 [64], P('replica'), may hold values from 1 to 256
- guest_source: int32 [32], P(('replica', 'tensor')), may hold values from 0 to 7, as said below
- guest_pages: int32 [32, 2], P(('replica', 'tensor')), may hold values from 4 to 5, as said below
- guest_len: int32 [32], P(('replica', 'tensor')), may hold values from 1 to 256
- routes: int32 [96, 6], P('replica'), may hold values from 0 to 7, all different within a row
Outputs:
- layer_out: bfloat16 [96, 1536], P(('replica', 'tensor'))
Inputs may be any that keep to these rules, and one draw needn't show every extreme that they name: `page_table`: the home requests of one replica name different pages, together each of a device's first 4 pages exactly once. `guest_source`: never the guest's own replica; among the guests of one slot and one tensor index, each replica is named exactly once. `guest_pages`: each row names 2 different pages, none of them named by a home request, and guests of different slots name different pages.
All inputs are finite; a program needn't handle non-finite values.
Results may differ from a plain program's by a relative error of at most 0.022.
Values may be sent and summed in bfloat16 or wider, within the bound.
No kernel may reach another device: no remote copies, remote signals or barrier semaphores. Data moves between devices by JAX's collectives and lax.ppermute only.
A program may use at most 64 MiB of HBM per device.

v0:
```python
import functools

import jax
import jax.numpy as jnp
from jax import lax
from jax.experimental import pallas as pl
from jax.experimental.pallas import tpu as pltpu
from jax.sharding import PartitionSpec as P

HEADS = 12
KVH = 4
HD = 128
MOE_FF = 512
LANES = 128
SUB = 8
CORES = 2
FAR = 1024
EMPTY = -1e30
STEP = 16
MAXP = 2

VMEM = pl.BlockSpec(memory_space=pltpu.VMEM)
SMEM = pl.BlockSpec(memory_space=pltpu.SMEM)
ANY = pl.BlockSpec(memory_space=pl.ANY)
PARAMS = pltpu.CompilerParams(vmem_limit_bytes=16 * 2**20)


def resident(array):
    return pltpu.with_memory_space_constraint(array, pltpu.VMEM)


def far(array):
    return pltpu.with_memory_space_constraint(array, pltpu.HBM)


def normed(values, gain):
    inverse = lax.rsqrt(jnp.mean(values * values, axis=-1, keepdims=True) + 1e-05)
    return (values * inverse * gain).astype(jnp.bfloat16)


def ways(size):
    return [(chips, core) for chips in range(size // CORES) for core in range(CORES)][1:]


def target(me, size, way):
    chip = lax.rem(me // CORES + way[0], size // CORES)
    return chip * CORES + lax.rem(me + way[1], CORES)


def sender(me, size, way):
    chip = lax.rem(me // CORES + size // CORES - way[0], size // CORES)
    return chip * CORES + lax.rem(me + way[1], CORES)


def senders(me, size):
    return [me] + [sender(me, size, way) for way in ways(size)]


def targets(me, size):
    return [me] + [target(me, size, way) for way in ways(size)]


def exchanged(blocks):
    size = len(blocks)
    arrived = [blocks[0]]
    for way, block in zip(ways(size), blocks[1:]):
        pairs = []
        for me in range(size):
            chip = (me // CORES + way[0]) % (size // CORES)
            pairs.append((me, chip * CORES + (me + way[1]) % CORES))
        arrived.append(lax.ppermute(block, "tensor", pairs))
    return arrived


def to_step(rows):
    extra = -rows.shape[0] % STEP
    if not extra:
        return rows
    filler = jnp.zeros((extra, rows.shape[1]), jnp.float32)
    return jnp.concatenate([rows.astype(jnp.float32), filler], axis=0).astype(rows.dtype)


def lanes_of(numbers, lane):
    row = jnp.zeros(lane.shape, jnp.float32)
    for place, number in enumerate(numbers):
        row = jnp.where(lane == place, number.astype(jnp.float32), row)
    return row


def at_lane(rows, lane, place):
    return jnp.sum(jnp.where(lane == place, rows, 0.0), axis=-1, keepdims=True)


def across(block, size):
    arrived = [block]
    for chips in range(1, size // CORES):
        pairs = [(me, (me + chips * CORES) % size) for me in range(size)]
        arrived.append(lax.ppermute(block, "tensor", pairs))
    return arrived


def page_hits(plan, pages):
    return [jnp.where(plan[place : place + 1] == pages, 1.0, 0.0) for place in range(MAXP)]


def offer_kernel(tokens, paths, pages, table, lens, packed, *refs):
    offers, homes, plan, tail_out, rows, paths_s, pages_s, table_v, lens_v, sems = refs
    pairs = [
        (tokens, rows),
        (paths, paths_s),
        (pages, pages_s),
        (table, table_v),
        (lens, lens_v.at[0]),
    ]
    copies = [pltpu.make_async_copy(*pair, sems.at[i]) for i, pair in enumerate(pairs)]
    for copy in copies:
        copy.start()
    for copy in copies:
        copy.wait()
    me = lax.axis_index("tensor")
    rows_dev, width = rows.shape
    top = paths.shape[0]
    lane = lax.broadcasted_iota(jnp.int32, (1, LANES), 1)
    wide = rows[...].astype(jnp.float32)
    tails = []
    for slot in range(rows_dev):
        numbers = [paths_s[place, me * rows_dev + slot] for place in range(top)]
        if slot == rows_dev - 1:
            numbers += [packed[0] % FAR]
            numbers += [pages_s[0, place] for place in range(MAXP)]
            numbers += [packed[0] // FAR]
        tails.append(lanes_of(numbers, lane))
    tail_out[...] = tails[-1]
    full = jnp.concatenate([wide, jnp.concatenate(tails, axis=0)], axis=1)
    homes[...] = full[:-1].astype(jnp.bfloat16)
    guest = jnp.concatenate(
        [wide[-1:], tails[-1], jnp.zeros((1, LANES), jnp.float32)], axis=1
    )
    half = guest.shape[1] // 2
    block = jnp.concatenate([guest[:, :half], guest[:, half:]], axis=0).astype(jnp.bfloat16)
    for place in range(offers.shape[0]):
        offers[place] = block

    count = table.shape[1]
    npages = plan.shape[0]
    size = count * MAXP // (npages - MAXP)
    filler = jnp.zeros((1, LANES - count), jnp.float32)
    spots = lane - count
    lines = []
    for place in range(MAXP):
        ids = table_v[place : place + 1].astype(jnp.float32)
        ids = jnp.concatenate([ids, filler], axis=1)
        guests = (spots * npages + npages - MAXP + place).astype(jnp.float32)
        guests = jnp.where(spots < size, guests, -1.0)
        lines.append(jnp.where(spots < 0, ids, guests))
    lines.append(jnp.concatenate([lens_v[...].astype(jnp.float32), filler], axis=1))
    lines.append(jnp.zeros((npages - MAXP - 1, LANES), jnp.float32))
    plan[...] = jnp.concatenate(lines, axis=0)


def load_kernel(plans, *refs):
    sources, outs, sems = refs[1 : 1 + len(plans)], refs[1 + len(plans) : -1], refs[-1]
    copies = []

    def copy(source, out):
        copies.append(pltpu.make_async_copy(source, out, sems.at[len(copies)]))

    for (first, count, pieces), source, out in zip(plans, sources, outs):
        each = source.shape[0] // pieces if len(out.shape) == 4 else count // pieces
        for piece in range(pieces):
            lines = pl.ds(piece * each, each)
            if len(out.shape) == 4:
                for place in range(count):
                    columns = pl.ds((first + place) * LANES, LANES)
                    copy(source.at[lines, :, columns], out.at[place, lines])
            else:
                copy(source.at[pl.ds(first + piece * each, each)], out.at[lines])
    for made in copies:
        made.start()
    for made in copies:
        made.wait()


def loaded(after, *wanted):
    shapes, plans, copies = [], [], 0
    for array, first, count in wanted:
        if array.ndim == 3:
            shapes.append(shape((count,) + array.shape[:2] + (LANES,), array.dtype))
            plans.append((first, count, 2))
            copies += 2 * count
        else:
            shapes.append(shape((count, array.shape[1]), array.dtype))
            plans.append((first, count, 4))
            copies += 4
    parts = pl.pallas_call(
        functools.partial(load_kernel, tuple(plans)),
        out_shape=shapes,
        in_specs=[ANY] * (1 + len(wanted)),
        out_specs=[VMEM] * len(wanted),
        scratch_shapes=[pltpu.SemaphoreType.DMA((copies,))],
        compiler_params=PARAMS,
        cost_estimate=pl.CostEstimate(
            flops=0, bytes_accessed=sum(2 * part.size for part in shapes), transcendentals=0
        ),
        name="load",
    )(after, *[far(array) for array, _, _ in wanted])
    return [
        part.reshape(part.shape[0], -1, LANES) if part.ndim == 4 else part for part in parts
    ]


def project_kernel(size, npages, top, *refs):
    blocks, refs = refs[:size], refs[size:]
    offers, gain, weight, plan, rows_ref = refs[:5]
    outs = refs[5 : 5 + size]
    gathered, paged = refs[5 + size :]
    me = lax.axis_index("tensor")
    replica = lax.axis_index("replica").astype(jnp.float32)
    home_dev = blocks[0].shape[0]
    homes = size * home_dev
    width, columns = weight.shape
    for owner, block in zip(senders(me, size), blocks):
        gathered[pl.ds(owner, 1)] = block[...].astype(jnp.float32)[None]
    came = offers[...].astype(jnp.float32)
    half = came.shape[2]
    lane = lax.broadcasted_iota(jnp.int32, (1, 1, half), 2)
    spot = width + top + 1 + MAXP - half
    source = jnp.sum(jnp.where(lane == spot, came[:, 1:], 0.0), axis=2, keepdims=True)
    picked = jnp.where(source == replica, came, 0.0)
    picked = jnp.sum(picked.reshape(-1, size, 2, half), axis=0)
    for owner in range(size):
        rows_ref[owner * home_dev : (owner + 1) * home_dev] = gathered[owner]
        guest = jnp.concatenate([picked[owner, :1], picked[owner, 1:]], axis=1)
        rows_ref[homes + owner : homes + owner + 1] = guest[:, : width + LANES]
    norm = to_step(normed(rows_ref[:, :width], gain[...]))
    products = jnp.dot(norm, weight[...], preferred_element_type=jnp.float32)
    line = lax.broadcasted_iota(jnp.int32, (size * SUB, LANES), 0)
    ids = line // SUB * npages + line % SUB
    ids = jnp.where(line % SUB < npages, ids, -2).astype(jnp.float32)
    hits = sum(page_hits(plan[...], ids))[:, : norm.shape[0]]
    paged[...] = jnp.dot(
        hits.astype(jnp.bfloat16), products.astype(jnp.bfloat16), preferred_element_type=jnp.float32
    )
    for end, out in zip(targets(me, size), outs):
        start = pl.multiple_of(end * SUB, SUB)
        out[...] = paged[pl.ds(start, SUB)][:npages].astype(jnp.bfloat16)


def attend_kernel(size, top, *refs):
    blocks, refs = refs[:size], refs[size:]
    cache, rows_ref, plan_ref, _ = refs[:4]
    outs = refs[4 : 4 + size]
    gathered, terms = refs[4 + size :]
    me = lax.axis_index("tensor")
    npages, _, page_len, _ = cache.shape
    home_pages = npages - MAXP
    homes = home_pages // MAXP * size
    group = HEADS // KVH
    qwidth, kwidth = HEADS * HD, KVH * HD
    width = rows_ref.shape[1] - LANES
    for owner, block in zip(senders(me, size), blocks):
        gathered[pl.ds(owner, 1), :npages] = block[...].astype(jnp.float32)[None]
    joined = jnp.concatenate([gathered[owner] for owner in range(size)], axis=1)

    plan = plan_ref[...]
    line = lax.broadcasted_iota(jnp.int32, (SUB, LANES), 0)
    hits = page_hits(plan, (me * npages + line).astype(jnp.float32))
    left = sum(
        hit * (plan[MAXP : MAXP + 1] - float(place * page_len)) for place, hit in enumerate(hits)
    )
    left = jnp.sum(left, axis=1, keepdims=True)
    leads = jnp.sum(hits[0], axis=1, keepdims=True)
    tails = rows_ref[:, width:]
    place = lax.broadcasted_iota(jnp.int32, tails.shape, 0)
    numbers = jnp.sum(jnp.where(place == homes + me, tails, 0.0), axis=0, keepdims=True)
    lane = lax.broadcasted_iota(jnp.int32, (1, LANES), 1)
    near_len = at_lane(numbers, lane, top)
    line = line[:, :1]
    near_left, near_lead = jnp.zeros((SUB, 1), jnp.float32), None
    for place in range(MAXP):
        named = at_lane(numbers, lane, top + 1 + place) == line.astype(jnp.float32)
        near_left = jnp.where(named, near_len - float(place * page_len), near_left)
        if place == 0:
            near_lead = jnp.where(named, 1.0, 0.0)
    left = jnp.where(line < home_pages, left, near_left)
    leads = jnp.where(line < home_pages, leads, near_lead)
    row = lax.broadcasted_iota(jnp.int32, (SUB, npages * page_len), 0)
    spot = lax.broadcasted_iota(jnp.int32, (SUB, npages * page_len), 1)
    inside = (spot - row * page_len).astype(jnp.float32)
    usable = jnp.where((inside >= 0.0) & (inside < jnp.minimum(left, float(page_len))), 1.0, 0.0)
    usable = jnp.concatenate([usable] * HEADS, axis=0) > 0.5
    leads = jnp.concatenate([leads] * HEADS, axis=0) > 0.5

    query = jnp.concatenate([joined[:, h * HD : (h + 1) * HD] for h in range(HEADS)], axis=0)
    fresh_key, fresh_value = [
        jnp.concatenate(
            [joined[:, start + h // group * HD : start + (h // group + 1) * HD] for h in range(HEADS)],
            axis=0,
        )
        for start in (qwidth, qwidth + kwidth)
    ]
    lines = group * SUB
    narrow = query.astype(jnp.bfloat16)
    scores = []
    for kv in range(KVH):
        keys = cache[:, 0, :, kv * HD : (kv + 1) * HD].reshape(npages * page_len, HD)
        scores.append(
            lax.dot_general(
                narrow[kv * lines : (kv + 1) * lines],
                keys,
                (((1,), (1,)), ((), ())),
                preferred_element_type=jnp.float32,
            )
        )
    scores = jnp.concatenate(scores, axis=0) * HD ** (-0.5)
    scores = jnp.where(usable, scores, EMPTY)
    own = jnp.sum(query * fresh_key, axis=-1, keepdims=True) * HD ** (-0.5)
    own = jnp.where(leads, own, EMPTY)
    peak = jnp.maximum(jnp.max(scores, axis=-1, keepdims=True), own)
    weights = jnp.where(usable, jnp.exp(scores - peak), 0.0)
    newest = jnp.where(leads, jnp.exp(own - peak), 0.0)
    total = jnp.sum(weights, axis=-1, keepdims=True) + newest
    narrow = weights.astype(jnp.bfloat16)
    summed = []
    for kv in range(KVH):
        values = cache[:, 1, :, kv * HD : (kv + 1) * HD].reshape(npages * page_len, HD)
        summed.append(
            jnp.dot(
                narrow[kv * lines : (kv + 1) * lines], values, preferred_element_type=jnp.float32
            )
        )
    summed = jnp.concatenate(summed, axis=0) + newest * fresh_value
    used = total > 0.0
    safe = jnp.where(used, total, 1.0)
    mixed = summed / safe
    level = jnp.where(used, peak + jnp.log(safe), EMPTY)
    lane = lax.broadcasted_iota(jnp.int32, (SUB, LANES), 1)
    levels = jnp.zeros((SUB, LANES), jnp.float32)
    for h in range(HEADS):
        levels = jnp.where(lane % STEP == h, level[h * SUB : (h + 1) * SUB], levels)
    upper = levels.astype(jnp.bfloat16).astype(jnp.float32)
    rest = levels - upper
    middle = rest.astype(jnp.bfloat16).astype(jnp.float32)
    levels = jnp.where(lane < STEP, upper, jnp.where(lane < 2 * STEP, middle, rest - middle))
    levels = jnp.where(lane < 3 * STEP, levels, 0.0)
    mixes = jnp.concatenate([mixed[h * SUB : (h + 1) * SUB] for h in range(HEADS)], axis=1)
    chips = size // CORES
    part = qwidth // chips
    for chip in range(chips):
        terms[chip] = jnp.concatenate([mixes[:, chip * part : (chip + 1) * part], levels], axis=1)
    for end, out in zip(targets(me, size), outs):
        out[...] = terms[pl.ds(end // CORES, 1)][0, :npages].astype(jnp.bfloat16)


def out_kernel(size, npages, *refs):
    blocks, refs = refs[:size], refs[size:]
    weight, mate_weight, plan, _, out = refs
    me = lax.axis_index("tensor")
    part = CORES * weight.shape[0]
    terms, ids = [], []
    line = lax.broadcasted_iota(jnp.int32, (SUB, LANES), 0)
    filler = jnp.zeros((SUB - npages, part + LANES), jnp.float32)
    for owner, block in zip(senders(me, size), blocks):
        terms += [block[...].astype(jnp.float32), filler]
        ids.append(jnp.where(line < npages, owner * npages + line, -2))
    terms = jnp.concatenate(terms, axis=0).astype(jnp.bfloat16)
    ids = jnp.concatenate(ids, axis=0).astype(jnp.float32)
    spread = lax.broadcasted_iota(jnp.int32, (LANES, part), 0)
    head = (lax.broadcasted_iota(jnp.int32, (LANES, part), 1) + me // CORES * part) // HD
    spread = jnp.where((spread % STEP == head) & (spread < 3 * STEP), 1.0, 0.0)
    spread = spread.astype(jnp.bfloat16)
    count = out.shape[0]
    rows = count + -count % STEP
    mixes, levels = [], []
    for hit in page_hits(plan[...], ids):
        picked = lax.dot_general(
            hit[:, :rows].astype(jnp.bfloat16),
            terms,
            (((0,), (0,)), ((), ())),
            preferred_element_type=jnp.float32,
        )
        mixes.append(picked[:, :part])
        levels.append(
            jnp.dot(
                picked[:, part:].astype(jnp.bfloat16), spread, preferred_element_type=jnp.float32
            )
        )
    highest = functools.reduce(jnp.maximum, levels)
    factors = [jnp.exp(level - highest) for level in levels]
    mixed = sum(mix * factor for mix, factor in zip(mixes, factors)) / sum(factors)
    halves = mixed[:, : part // CORES], mixed[:, part // CORES :]
    first = lax.rem(me, CORES) == 0
    own = jnp.where(first, halves[0], halves[1]).astype(jnp.bfloat16)
    other = jnp.where(first, halves[1], halves[0]).astype(jnp.bfloat16)
    products = jnp.dot(own, weight[...], preferred_element_type=jnp.float32)
    products += jnp.dot(other, mate_weight[...], preferred_element_type=jnp.float32)
    out[...] = products[:count].astype(jnp.bfloat16)


def expert_kernel(size, top, experts, parts, lows, *refs):
    chips = size // CORES
    sums, refs = refs[:chips], refs[chips:]
    rows_ref, gain, router = refs[:3]
    gate_up, refs = refs[3 : 3 + parts], refs[3 + parts :]
    down, refs = refs[:lows], refs[lows:]
    units = sum(piece.shape[0] for piece in down)
    homes, guests, finished, ends_ref = refs[:size], refs[size], refs[size + 1], refs[size + 2]
    me = lax.axis_index("tensor")
    count = rows_ref.shape[0]
    width = rows_ref.shape[1] - LANES
    rows_dev = count // size
    total = functools.reduce(jnp.add, [piece[...].astype(jnp.float32) for piece in sums])
    hidden = (rows_ref[:, :width] + total).astype(jnp.bfloat16).astype(jnp.float32)
    norm = normed(hidden, gain[...])
    lane = lax.broadcasted_iota(jnp.int32, (count, LANES), 1)
    numbers = rows_ref[:, width:]
    logits = lax.dot_general(
        norm, router[...], (((1,), (1,)), ((), ())), preferred_element_type=jnp.float32
    )
    logits = jnp.concatenate(
        [logits, jnp.zeros((count, LANES - experts), jnp.float32)], axis=1
    )
    routed = jnp.zeros((count, LANES), jnp.float32)
    for place in range(top):
        route = at_lane(numbers, lane, place)
        routed = jnp.where(lane.astype(jnp.float32) == route, 1.0, routed)
    logits = jnp.where(routed > 0.5, logits, EMPTY)
    shares = jnp.where(
        routed > 0.5, jnp.exp(logits - jnp.max(logits, axis=-1, keepdims=True)), 0.0
    )
    shares = shares / jnp.sum(shares, axis=-1, keepdims=True)

    here = lax.broadcasted_iota(jnp.int32, (LANES, 2 * LANES), 0)
    there = lax.broadcasted_iota(jnp.int32, (LANES, 2 * LANES), 1)
    evens = jnp.where(there == 2 * here, 1.0, 0.0).astype(jnp.bfloat16)
    odds = jnp.where(there == 2 * here + 1, 1.0, 0.0).astype(jnp.bfloat16)
    wide = to_step(norm)
    padded = wide.shape[0]
    blocks = width // LANES
    tall = jnp.concatenate([wide[:, b * LANES : (b + 1) * LANES] for b in range(blocks)], axis=0)
    to_gate = jnp.dot(tall, evens, preferred_element_type=jnp.float32).astype(jnp.bfloat16)
    to_up = jnp.dot(tall, odds, preferred_element_type=jnp.float32).astype(jnp.bfloat16)
    left = []
    for b in range(blocks):
        lines = slice(b * padded, (b + 1) * padded)
        left.append(jnp.concatenate([to_gate[lines], to_up[lines]], axis=0))
    left = jnp.concatenate(left, axis=1)
    both = []
    for piece in gate_up:
        right = jnp.concatenate([piece[place] for place in range(piece.shape[0])], axis=1)
        both.append(jnp.dot(left, right, preferred_element_type=jnp.float32))
    both = jnp.concatenate(both, axis=1)
    gate, up = both[:count], both[padded : padded + count]
    activated = gate / (1.0 + jnp.exp(-gate)) * up
    step = min(units, MOE_FF)
    scaled = []
    for start in range(0, units, step):
        expert = (me * units + start) // MOE_FF
        share = at_lane(shares, lane, expert)
        scaled.append(activated[:, start : start + step] * share)
    scaled = jnp.concatenate(scaled, axis=1).astype(jnp.bfloat16)
    partial, start = 0.0, 0
    for piece in down:
        left = scaled[:, start : start + piece.shape[0]]
        partial += jnp.dot(left, piece[...], preferred_element_type=jnp.float32)
        start += piece.shape[0]
    home_dev = rows_dev - 1
    first = size * home_dev
    for owner in range(size):
        lines = slice(owner * home_dev, (owner + 1) * home_dev)
        mine = jnp.where(me == owner, 1.0, 0.0)
        finished[owner] = partial[lines] + hidden[lines] * mine
        line = slice(first + owner, first + owner + 1)
        ends_ref[owner : owner + 1] = partial[line] + hidden[line] * mine
    for end, out in zip(targets(me, size), homes):
        out[...] = finished[pl.ds(end, 1)][0].astype(jnp.bfloat16)
    half = width // 2
    for owner in range(size):
        guest = ends_ref[owner : owner + 1]
        block = jnp.concatenate([guest[:, :half], guest[:, half:]], axis=0).astype(jnp.bfloat16)
        for place in range(owner, guests.shape[0], size):
            guests[place] = block


def finish_kernel(size, spot, *refs):
    pieces, refs = refs[:size], refs[size:]
    guests, tail, out = refs
    homes = functools.reduce(jnp.add, [piece[...].astype(jnp.float32) for piece in pieces])
    came = guests[...].astype(jnp.float32)
    lane = lax.broadcasted_iota(jnp.int32, (1, LANES), 1)
    source = at_lane(tail[...], lane, spot).reshape(1, 1, 1)
    place = lax.broadcasted_iota(jnp.int32, (came.shape[0], 1, 1), 0) // size
    guest = jnp.sum(jnp.where(place.astype(jnp.float32) == source, came, 0.0), axis=0)
    guest = jnp.concatenate([guest[:1], guest[1:]], axis=1)
    out[...] = jnp.concatenate([homes, guest], axis=0).astype(jnp.bfloat16)


def shape(dims, dtype=jnp.float32):
    return jax.ShapeDtypeStruct(dims, dtype)


def shards(
    tokens,
    attn_gain,
    qkv_weight,
    out_weight,
    moe_gain,
    router,
    expert_gate_up,
    expert_down,
    kv_cache,
    page_table,
    home_len,
    guest_source,
    guest_pages,
    guest_len,
    routes,
):
    size = lax.axis_size("tensor")
    replicas = lax.axis_size("replica")
    rows_dev, width = tokens.shape
    npages = kv_cache.shape[0]
    top = routes.shape[1]
    units = expert_down.shape[0]
    part = out_weight.shape[0]
    columns = qkv_weight.shape[1]
    count = size * rows_dev
    home_dev = rows_dev - 1
    wide = width + LANES
    everyone = size * replicas
    blocks = units // LANES
    gate_up, down = [], []

    def load_more(after, ups, downs):
        first, last = ups[0] * blocks // 8, ups[1] * blocks // 8
        wanted = []
        if last > first:
            wanted.append((expert_gate_up, first, last - first))
        if downs[1] > downs[0]:
            wanted.append((expert_down, downs[0] * units // 8, (downs[1] - downs[0]) * units // 8))
        if not wanted:
            return after
        got = loaded(after, *wanted)
        for part in got:
            (gate_up if part.ndim == 3 else down).append(part)
        return got[0]

    packed = guest_source * FAR + guest_len
    offers, homes, plan, tail = pl.pallas_call(
        offer_kernel,
        out_shape=[
            shape((everyone, 2, (wide + LANES) // 2), jnp.bfloat16),
            shape((home_dev, wide), jnp.bfloat16),
            shape((npages, LANES)),
            shape((1, LANES)),
        ],
        in_specs=[ANY] * 5 + [SMEM],
        out_specs=[VMEM] * 4,
        scratch_shapes=[
            pltpu.VMEM(tokens.shape, tokens.dtype),
            pltpu.SMEM(routes.T.shape, jnp.int32),
            pltpu.SMEM(guest_pages.shape, jnp.int32),
            pltpu.VMEM(page_table.T.shape, jnp.int32),
            pltpu.VMEM((1,) + home_len.shape, jnp.int32),
            pltpu.SemaphoreType.DMA((5,)),
        ],
        compiler_params=PARAMS,
        name="offer",
    )(far(tokens), far(routes.T), far(guest_pages), far(page_table.T), far(home_len), packed)
    came = lax.all_to_all(offers, ("replica", "tensor"), 0, 0, tiled=True)
    messages = exchanged([homes] * size)
    (qkv_near,) = loaded(homes, (qkv_weight, 0, width))

    rows, *projected = pl.pallas_call(
        functools.partial(project_kernel, size, npages, top),
        out_shape=[shape((count, wide))] + [shape((npages, columns), jnp.bfloat16)] * size,
        in_specs=[VMEM] * (size + 4),
        out_specs=[VMEM] * (size + 1),
        scratch_shapes=[
            pltpu.VMEM((size, home_dev, wide), jnp.float32),
            pltpu.VMEM((size * SUB, columns), jnp.float32),
        ],
        compiler_params=PARAMS,
        name="project",
    )(
        *messages,
        came,
        attn_gain.reshape(1, width),
        resident(qkv_near),
        plan,
    )
    joined = exchanged(projected)

    before = load_more(rows, (0, 2), (0, 2))
    late, _ = lax.optimization_barrier((out_weight, rows))
    out_mate = lax.ppermute(late, "tensor", [(me, me ^ 1) for me in range(size)])
    terms = pl.pallas_call(
        functools.partial(attend_kernel, size, top),
        out_shape=[shape((npages, CORES * part + LANES), jnp.bfloat16)] * size,
        in_specs=[VMEM] * (size + 3) + [ANY],
        out_specs=[VMEM] * size,
        scratch_shapes=[
            pltpu.VMEM((size, SUB, columns), jnp.float32),
            pltpu.VMEM((size // CORES, SUB, CORES * part + LANES), jnp.float32),
        ],
        compiler_params=PARAMS,
        name="attend",
    )(*joined, resident(kv_cache), rows, plan, before)
    arrived = exchanged(terms)

    before = load_more(terms[0], (2, 5), (2, 4))
    partial = pl.pallas_call(
        functools.partial(out_kernel, size, npages),
        out_shape=shape((count, width), jnp.bfloat16),
        in_specs=[VMEM] * (size + 3) + [ANY],
        out_specs=VMEM,
        compiler_params=PARAMS,
        name="out",
    )(*arrived, resident(out_weight), resident(out_mate), plan, before)
    sums = across(partial, size)

    load_more(partial, (5, 8), (4, 8))
    *pieces, guests = pl.pallas_call(
        functools.partial(
            expert_kernel, size, top, router.shape[1], len(gate_up), len(down)
        ),
        out_shape=[shape((home_dev, width), jnp.bfloat16)] * size
        + [shape((everyone, 2, width // 2), jnp.bfloat16)],
        in_specs=[VMEM] * (len(sums) + 3 + len(gate_up) + len(down)),
        out_specs=[VMEM] * (size + 1),
        scratch_shapes=[
            pltpu.VMEM((size, home_dev, width), jnp.float32),
            pltpu.VMEM((size, width), jnp.float32),
        ],
        compiler_params=PARAMS,
        name="experts",
    )(
        *sums,
        rows,
        moe_gain.reshape(1, width),
        router.T,
        *[resident(piece) for piece in gate_up + down],
    )
    guests = lax.all_to_all(guests, ("replica", "tensor"), 0, 0, tiled=True)
    pieces = exchanged(pieces)
    return pl.pallas_call(
        functools.partial(finish_kernel, size, top + 1 + MAXP),
        out_shape=shape((rows_dev, width), jnp.bfloat16),
        in_specs=[VMEM] * (size + 2),
        out_specs=VMEM,
        compiler_params=PARAMS,
        name="finish",
    )(*pieces, guests, tail)


def solution(mesh):
    placed = (
        P(("replica", "tensor"), None),
        P(),
        P(None, "tensor"),
        P("tensor", None),
        P(),
        P(),
        P(None, None, "tensor"),
        P("tensor", None),
        P(("replica", "tensor"), None, None, None),
        P("replica", None),
        P("replica"),
        P(("replica", "tensor")),
        P(("replica", "tensor"), None),
        P(("replica", "tensor")),
        P("replica", None),
    )
    return jax.shard_map(
        shards,
        mesh=mesh,
        in_specs=placed,
        out_specs=P(("replica", "tensor"), None),
        check_vma=False,
    )
```

profile of v0, /device:TPU:0, one launch (start us, length us, event | category | flops | bytes accessed | tf_op | source)
XLA Modules:
  0.0 47.7 jit_solution(11576684307657754440)
XLA Ops:
  1.3 1.6 %offer.1 = (bf16[32,2,896]{2,1,0:T(2,128)(2,1)}, bf16[2,1664]{1,0:T(2,128)(2,1)S(1)}, f32[6,128]{1,0:T(8,128)S(1)}, f32[1,128]{1,0:T(1,128)S(1)}) custom-call(bf16[3,1536]{1,0:T(4,128)(2,1)} %tokens.1, s32[6,12]{1,0:T(8,128)} %bitcast.12, s32[1,2]{1,0:T(1,128)} %pages.1, s32[2,8]{1,0:T(2,128)} %bitcast.13, s32[8]{0:T(128)} %lens.1, s32[1]{0:T(128)S(6)} %add.3.packed), custom_call_target="tpu_custom_call" | custom-call | tf_op jit(solution)/shard_map/offer/pallas_call | solution.py:549
  2.9 7.3 %all-to-all-start = ((bf16[32,2,896]{2,1,0:T(2,128)(2,1)}), bf16[32,2,896]{2,1,0:T(2,128)(2,1)S(1)}, u32[]{:S(2)}, u32[]{:S(2)}) async-start(bf16[32,2,896]{2,1,0:T(2,128)(2,1)} %get-tuple-element.31), calls=%async_computation | async-start | bytes 229376 | tf_op jit(solution)/shard_map/all_to_all | solution.py:570
  10.2 1.6 %collective-permute-start.2 = (bf16[2,1664]{1,0:T(2,128)(2,1)S(1)}, bf16[2,1664]{1,0:T(2,128)(2,1)S(1)}, u32[]{:S(2)}, u32[]{:S(2)}) collective-permute-start(bf16[2,1664]{1,0:T(2,128)(2,1)S(1)} %get-tuple-element.30.refs_0_), channel_id=1, source_target_pairs={{0,3},{1,2},{2,1},{3,0},{4,7},{5,6},{6,5},{7,4},{8,11},{9,10},{10,... | collective-permute-start | bytes 19976 | tf_op jit(solution)/shard_map/ppermute | solution.py:71
  11.8 0.4 collective-permute-start.1
  12.1 0.0 collective-permute-start
  12.2 0.7 %reshape.15.refs_5_ = f32[1,1536]{1,0:T(1,128)S(1)} reshape(f32[1536]{0:T(1024)} %param.16) | data formatting | bytes 12288 | tf_op jit(solution)/shard_map/reshape | solution.py:588
  12.9 1.5 %load.4.refs_6_ = bf16[1536,640]{1,0:T(8,128)(2,1)S(1)} custom-call(bf16[2,1664]{1,0:T(2,128)(2,1)S(1)} %get-tuple-element.30.refs_0_, bf16[1536,640]{1,0:T(8,128)(2,1)} %refs_1_.4), custom_call_target="tpu_custom_call" | custom-call | bytes 1966080 | tf_op jit(solution)/shard_map/load/pallas_call | solution.py:195
  14.4 0.0 copy-start.1
  14.4 0.0 collective-permute-done.2.refs_3_
  14.4 1.0 %collective-permute-done.1.refs_2_ = bf16[2,1664]{1,0:T(2,128)(2,1)S(1)} collective-permute-done((bf16[2,1664]{1,0:T(2,128)(2,1)S(1)}, bf16[2,1664]{1,0:T(2,128)(2,1)S(1)}, u32[]{:S(2)}, u32[]{:S(2)}) %collective-permute-start.1) | collective-permute-done | bytes 6688 | tf_op jit(solution)/shard_map/ppermute | solution.py:71
  15.4 0.0 collective-permute-done.refs_1_
  15.4 2.8 %all-to-all-done.refs_4_ = bf16[32,2,896]{2,1,0:T(2,128)(2,1)S(1)} async-done(((bf16[32,2,896]{2,1,0:T(2,128)(2,1)}), bf16[32,2,896]{2,1,0:T(2,128)(2,1)S(1)}, u32[]{:S(2)}, u32[]{:S(2)}) %all-to-all-start) | async-done | bytes 114720 | tf_op jit(solution)/shard_map/all_to_all | solution.py:570
  18.2 0.8 %project.1 = (f32[12,1664]{1,0:T(8,128)S(1)}, bf16[6,640]{1,0:T(8,128)(2,1)S(1)}, bf16[6,640]{1,0:T(8,128)(2,1)S(1)}, bf16[6,640]{1,0:T(8,128)(2,1)S(1)}, bf16[6,640]{1,0:T(8,128)(2,1)S(1)}) custom-call(bf16[2,1664]{1,0:T(2,128)(2,1)S(1)} %get-tuple-element.30.refs_0_, bf16[2,1664]{1,0:T(2,128)(2,1)S(1)} %collective-permute-done.refs_1_, ...), custom_call_target="tpu_custom_call" | custom-call | tf_op jit(solution)/shard_map/project/pallas_call | solution.py:574
  19.0 0.0 copy-done.1
  19.0 0.2 collective-permute-start.9
  19.2 0.3 collective-permute-start.3
  19.6 0.4 collective-permute-start.4
  20.0 1.1 %collective-permute-start.5 = (bf16[6,640]{1,0:T(8,128)(2,1)S(1)}, bf16[6,640]{1,0:T(8,128)(2,1)S(1)}, u32[]{:S(2)}, u32[]{:S(2)}) collective-permute-start(bf16[6,640]{1,0:T(8,128)(2,1)S(1)} %get-tuple-element.36), channel_id=1, source_target_pairs={{0,3},{1,2},{2,1},{3,0},{4,7},{5,6},{6,5},{7,4},{8,11},{9,10},{10,... | collective-permute-start | bytes 23048 | tf_op jit(solution)/shard_map/ppermute | solution.py:71
  21.1 1.7 %load.5 = (bf16[2,1536,2,128]{3,2,1,0:T(2,128)(2,1)S(1)}, bf16[256,1536]{1,0:T(8,128)(2,1)S(1)}) custom-call(f32[12,1664]{1,0:T(8,128)S(1)} %get-tuple-element.37.refs_0_.refs_5_.refs_2_, bf16[1536,2,1024]{2,1,0:T(2,128)(2,1)} %refs_1_.7, bf16[1024,1536]{1,0:T(8,128)(2,1)} %refs_2_.5), custom_call_target="tpu_custom_call" | custom-call | bytes 2359296 | tf_op jit(solution)/shard_map/load/pallas_call | solution.py:195
  22.8 0.0 collective-permute-done.3.refs_1_
  22.8 0.4 collective-permute-done.4.refs_2_
  23.3 0.0 collective-permute-done.5.refs_3_
  23.3 0.0 copy-done
  23.3 0.7 %attend.1 = (bf16[6,896]{1,0:T(8,128)(2,1)S(1)}, bf16[6,896]{1,0:T(8,128)(2,1)S(1)}, bf16[6,896]{1,0:T(8,128)(2,1)S(1)}, bf16[6,896]{1,0:T(8,128)(2,1)S(1)}) custom-call(bf16[6,640]{1,0:T(8,128)(2,1)S(1)} %get-tuple-element.33.refs_0_, bf16[6,640]{1,0:T(8,128)(2,1)S(1)} %collective-permute-done.3.refs_1_, bf16[6,640]{1,0:T(8,128)(2,1)S(1)} %collective-permute-done.4.refs_2_, ...), custom_call_target="tpu_custom_call" | custom-call | tf_op jit(solution)/shard_map/attend/pallas_call | solution.py:597
  24.0 0.3 collective-permute-start.6
  24.3 1.4 %collective-permute-start.7 = (bf16[6,896]{1,0:T(8,128)(2,1)S(1)}, bf16[6,896]{1,0:T(8,128)(2,1)S(1)}, u32[]{:S(2)}, u32[]{:S(2)}) collective-permute-start(bf16[6,896]{1,0:T(8,128)(2,1)S(1)} %get-tuple-element.41), channel_id=1, source_target_pairs={{0,2},{1,3},{2,0},{3,1},{4,6},{5,7},{6,4},{7,5},{8,10},{9,11},{10,... | collective-permute-start | bytes 32264 | tf_op jit(solution)/shard_map/ppermute | solution.py:71
  25.7 0.2 collective-permute-start.8
  25.9 1.9 %load.6 = (bf16[3,1536,2,128]{3,2,1,0:T(2,128)(2,1)S(1)}, bf16[256,1536]{1,0:T(8,128)(2,1)S(1)}) custom-call(bf16[6,896]{1,0:T(8,128)(2,1)S(1)} %get-tuple-element.39.refs_0_, bf16[1536,2,1024]{2,1,0:T(2,128)(2,1)} %refs_1_.7, bf16[1024,1536]{1,0:T(8,128)(2,1)} %refs_2_.5), custom_call_target="tpu_custom_call" | custom-call | bytes 3145728 | tf_op jit(solution)/shard_map/load/pallas_call | solution.py:195
  27.9 0.0 collective-permute-done.6.refs_1_
  27.9 0.1 collective-permute-done.7.refs_2_
  28.0 0.9 %collective-permute-done.8.refs_3_ = bf16[6,896]{1,0:T(8,128)(2,1)S(1)} collective-permute-done((bf16[6,896]{1,0:T(8,128)(2,1)S(1)}, bf16[6,896]{1,0:T(8,128)(2,1)S(1)}, u32[]{:S(2)}, u32[]{:S(2)}) %collective-permute-start.8) | collective-permute-done | bytes 10784 | tf_op jit(solution)/shard_map/ppermute | solution.py:71
  28.9 0.0 collective-permute-done.9.refs_5_
  28.9 0.8 %out.1.refs_0_ = bf16[12,1536]{1,0:T(8,128)(2,1)S(1)} custom-call(bf16[6,896]{1,0:T(8,128)(2,1)S(1)} %get-tuple-element.39.refs_0_, bf16[6,896]{1,0:T(8,128)(2,1)S(1)} %collective-permute-done.6.refs_1_, bf16[6,896]{1,0:T(8,128)(2,1)S(1)} %collective-permute-done.7.refs_2_, bf16[6,896]{1,0:T(8,128)(2,1)S(1)} %collective-permute-done.8.refs_3_, ...), custom_call_target="tpu_custom_call" | custom-call | tf_op jit(solution)/shard_map/out/pallas_call | solution.py:612
  29.7 0.7 %collective-permute-start.10 = (bf16[12,1536]{1,0:T(8,128)(2,1)S(1)}, bf16[12,1536]{1,0:T(8,128)(2,1)S(1)}, u32[]{:S(2)}, u32[]{:S(2)}) collective-permute-start(bf16[12,1536]{1,0:T(8,128)(2,1)S(1)} %out.1.refs_0_), channel_id=1, source_target_pairs={{0,2},{1,3},{2,0},{3,1},{4,6},{5,7},{6,4},{7,5},{8,10},{9,11},{10,... | collective-permute-start | bytes 110600 | tf_op jit(solution)/shard_map/ppermute | solution.py:98
  30.5 0.0 copy-done.3
  30.5 0.0 copy-start.2
  30.5 2.2 %load.7 = (bf16[3,1536,2,128]{3,2,1,0:T(2,128)(2,1)S(1)}, bf16[512,1536]{1,0:T(8,128)(2,1)S(1)}) custom-call(bf16[12,1536]{1,0:T(8,128)(2,1)S(1)} %out.1.refs_0_, bf16[1536,2,1024]{2,1,0:T(2,128)(2,1)} %refs_1_.7, bf16[1024,1536]{1,0:T(8,128)(2,1)} %refs_2_.5), custom_call_target="tpu_custom_call" | custom-call | bytes 3932160 | tf_op jit(solution)/shard_map/load/pallas_call | solution.py:195
  32.7 1.1 %collective-permute-done.10.refs_1_ = bf16[12,1536]{1,0:T(8,128)(2,1)S(1)} collective-permute-done((bf16[12,1536]{1,0:T(8,128)(2,1)S(1)}, bf16[12,1536]{1,0:T(8,128)(2,1)S(1)}, u32[]{:S(2)}, u32[]{:S(2)}) %collective-permute-start.10) | collective-permute-done | bytes 36896 | tf_op jit(solution)/shard_map/ppermute | solution.py:98
  33.8 2.7 %experts.1 = (bf16[2,1536]{1,0:T(2,128)(2,1)S(1)}, bf16[2,1536]{1,0:T(2,128)(2,1)S(1)}, bf16[2,1536]{1,0:T(2,128)(2,1)S(1)}, bf16[2,1536]{1,0:T(2,128)(2,1)S(1)}, bf16[32,2,768]{2,1,0:T(2,128)(2,1)}) custom-call(bf16[12,1536]{1,0:T(8,128)(2,1)S(1)} %out.1.refs_0_, bf16[12,1536]{1,0:T(8,128)(2,1)S(1)} %collective-permute-done.10.refs_1_, ...), custom_call_target="tpu_custom_call" | custom-call | tf_op jit(solution)/shard_map/experts/pallas_call | solution.py:623
  36.6 2.6 %all-to-all-start.1 = ((bf16[32,2,768]{2,1,0:T(2,128)(2,1)}), bf16[32,2,768]{2,1,0:T(2,128)(2,1)S(1)}, u32[]{:S(2)}, u32[]{:S(2)}) async-start(bf16[32,2,768]{2,1,0:T(2,128)(2,1)} %get-tuple-element.53), calls=%async_computation.1 | async-start | bytes 196608 | tf_op jit(solution)/shard_map/all_to_all | solution.py:644
  39.1 0.2 collective-permute-start.11
  39.3 1.7 %collective-permute-start.12 = (bf16[2,1536]{1,0:T(2,128)(2,1)S(1)}, bf16[2,1536]{1,0:T(2,128)(2,1)S(1)}, u32[]{:S(2)}, u32[]{:S(2)}) collective-permute-start(bf16[2,1536]{1,0:T(2,128)(2,1)S(1)} %get-tuple-element.51), channel_id=1, source_target_pairs={{0,2},{1,3},{2,0},{3,1},{4,6},{5,7},{6,4},{7,5},{8,10},{9,11},{10,... | collective-permute-start | bytes 18440 | tf_op jit(solution)/shard_map/ppermute | solution.py:71
  41.0 0.1 collective-permute-start.13
  41.1 0.0 collective-permute-done.11.refs_1_
  41.1 1.9 %collective-permute-done.12.refs_2_ = bf16[2,1536]{1,0:T(2,128)(2,1)S(1)} collective-permute-done((bf16[2,1536]{1,0:T(2,128)(2,1)S(1)}, bf16[2,1536]{1,0:T(2,128)(2,1)S(1)}, u32[]{:S(2)}, u32[]{:S(2)}) %collective-permute-start.12) | collective-permute-done | bytes 6176 | tf_op jit(solution)/shard_map/ppermute | solution.py:71
  43.0 1.1 %collective-permute-done.13.refs_3_ = bf16[2,1536]{1,0:T(2,128)(2,1)S(1)} collective-permute-done((bf16[2,1536]{1,0:T(2,128)(2,1)S(1)}, bf16[2,1536]{1,0:T(2,128)(2,1)S(1)}, u32[]{:S(2)}, u32[]{:S(2)}) %collective-permute-start.13) | collective-permute-done | bytes 6176 | tf_op jit(solution)/shard_map/ppermute | solution.py:71
  44.1 2.9 %all-to-all-done.1.refs_4_ = bf16[32,2,768]{2,1,0:T(2,128)(2,1)S(1)} async-done(((bf16[32,2,768]{2,1,0:T(2,128)(2,1)}), bf16[32,2,768]{2,1,0:T(2,128)(2,1)S(1)}, u32[]{:S(2)}, u32[]{:S(2)}) %all-to-all-start.1) | async-done | bytes 98336 | tf_op jit(solution)/shard_map/all_to_all | solution.py:644
  47.0 0.8 %finish.1 = bf16[3,1536]{1,0:T(4,128)(2,1)} custom-call(bf16[2,1536]{1,0:T(2,128)(2,1)S(1)} %get-tuple-element.49.refs_0_, bf16[2,1536]{1,0:T(2,128)(2,1)S(1)} %collective-permute-done.11.refs_1_, bf16[2,1536]{1,0:T(2,128)(2,1)S(1)} %collective-permute-done.12.refs_2_, bf16[2,1536]{1,0:T(2,128)(2,1)S(1)} %collective-permute-done.13.refs_3_, ...), custom_call_target="tpu_custom_call" | custom-call | tf_op jit(solution)/shard_map/finish/pallas_call | solution.py:646
  (4 shorter events, 0.0 us)
Async XLA Ops:
  2.9 15.3 %all-to-all-start = ((bf16[32,2,896]{2,1,0:T(2,128)(2,1)}), bf16[32,2,896]{2,1,0:T(2,128)(2,1)S(1)}, u32[]{:S(2)}, u32[]{:S(2)}) async-start(bf16[32,2,896]{2,1,0:T(2,128)(2,1)} %get-tuple-element.31), calls=%async_computation | async-start | bytes 229376 | tf_op jit(solution)/shard_map/all_to_all | solution.py:570
  10.2 4.2 %collective-permute-start.2 = (bf16[2,1664]{1,0:T(2,128)(2,1)S(1)}, bf16[2,1664]{1,0:T(2,128)(2,1)S(1)}, u32[]{:S(2)}, u32[]{:S(2)}) collective-permute-start(bf16[2,1664]{1,0:T(2,128)(2,1)S(1)} %get-tuple-element.30.refs_0_), channel_id=1, source_target_pairs={{0,3},{1,2},{2,1},{3,0},{4,7},{5,6},{6,5},{7,4},{8,11},{9,10},{10,... | collective-permute-start | bytes 19976 | tf_op jit(solution)/shard_map/ppermute | solution.py:71
  11.8 3.7 %collective-permute-start.1 = (bf16[2,1664]{1,0:T(2,128)(2,1)S(1)}, bf16[2,1664]{1,0:T(2,128)(2,1)S(1)}, u32[]{:S(2)}, u32[]{:S(2)}) collective-permute-start(bf16[2,1664]{1,0:T(2,128)(2,1)S(1)} %get-tuple-element.30.refs_0_), channel_id=1, source_target_pairs={{0,2},{1,3},{2,0},{3,1},{4,6},{5,7},{6,4},{7,5},{8,10},{9,11},{10,... | collective-permute-start | bytes 19976 | tf_op jit(solution)/shard_map/ppermute | solution.py:71
  12.1 3.3 %collective-permute-start = (bf16[2,1664]{1,0:T(2,128)(2,1)S(1)}, bf16[2,1664]{1,0:T(2,128)(2,1)S(1)}, u32[]{:S(2)}, u32[]{:S(2)}) collective-permute-start(bf16[2,1664]{1,0:T(2,128)(2,1)S(1)} %get-tuple-element.30.refs_0_), channel_id=1, source_target_pairs={{0,1},{1,0},{2,3},{3,2},{4,5},{5,4},{6,7},{7,6},{8,9},{9,8},{10,11... | collective-permute-start | bytes 19976 | tf_op jit(solution)/shard_map/ppermute | solution.py:71
  14.4 4.7 %copy-start.1 = (bf16[384,1536]{1,0:T(8,128)(2,1)S(1)}, bf16[384,1536]{1,0:T(8,128)(2,1)}, u32[]{:S(2)}) copy-start(bf16[384,1536]{1,0:T(8,128)(2,1)} %refs_4_.3) | copy-start | bytes 3538948
  19.0 9.8 %collective-permute-start.9 = (bf16[384,1536]{1,0:T(8,128)(2,1)S(1)}, bf16[384,1536]{1,0:T(8,128)(2,1)S(1)}, u32[]{:S(2)}, u32[]{:S(2)}) collective-permute-start(bf16[384,1536]{1,0:T(8,128)(2,1)S(1)} %copy-done.1), channel_id=1, source_target_pairs={{0,1},{1,0},{2,3},{3,2},{4,5},{5,4},{6,7},{7,6},{8,9},{9,8},{10,11... | collective-permute-start | bytes 3538952 | tf_op jit(solution)/shard_map/ppermute | solution.py:596
  19.2 3.6 %collective-permute-start.3 = (bf16[6,640]{1,0:T(8,128)(2,1)S(1)}, bf16[6,640]{1,0:T(8,128)(2,1)S(1)}, u32[]{:S(2)}, u32[]{:S(2)}) collective-permute-start(bf16[6,640]{1,0:T(8,128)(2,1)S(1)} %get-tuple-element.34), channel_id=1, source_target_pairs={{0,1},{1,0},{2,3},{3,2},{4,5},{5,4},{6,7},{7,6},{8,9},{9,8},{10,11... | collective-permute-start | bytes 23048 | tf_op jit(solution)/shard_map/ppermute | solution.py:71
  19.6 3.7 %collective-permute-start.4 = (bf16[6,640]{1,0:T(8,128)(2,1)S(1)}, bf16[6,640]{1,0:T(8,128)(2,1)S(1)}, u32[]{:S(2)}, u32[]{:S(2)}) collective-permute-start(bf16[6,640]{1,0:T(8,128)(2,1)S(1)} %get-tuple-element.35), channel_id=1, source_target_pairs={{0,2},{1,3},{2,0},{3,1},{4,6},{5,7},{6,4},{7,5},{8,10},{9,11},{10,... | collective-permute-start | bytes 23048 | tf_op jit(solution)/shard_map/ppermute | solution.py:71
  20.0 3.3 %copy-start = (bf16[6,2,128,512]{3,2,1,0:T(8,128)(2,1)S(1)}, bf16[6,2,128,512]{3,2,1,0:T(8,128)(2,1)}, u32[]{:S(2)}) copy-start(bf16[6,2,128,512]{3,2,1,0:T(8,128)(2,1)} %refs_4_.2) | copy-start | bytes 4718596
  20.0 3.3 %collective-permute-start.5 = (bf16[6,640]{1,0:T(8,128)(2,1)S(1)}, bf16[6,640]{1,0:T(8,128)(2,1)S(1)}, u32[]{:S(2)}, u32[]{:S(2)}) collective-permute-start(bf16[6,640]{1,0:T(8,128)(2,1)S(1)} %get-tuple-element.36), channel_id=1, source_target_pairs={{0,3},{1,2},{2,1},{3,0},{4,7},{5,6},{6,5},{7,4},{8,11},{9,10},{10,... | collective-permute-start | bytes 23048 | tf_op jit(solution)/shard_map/ppermute | solution.py:71
  24.0 3.8 %collective-permute-start.6 = (bf16[6,896]{1,0:T(8,128)(2,1)S(1)}, bf16[6,896]{1,0:T(8,128)(2,1)S(1)}, u32[]{:S(2)}, u32[]{:S(2)}) collective-permute-start(bf16[6,896]{1,0:T(8,128)(2,1)S(1)} %get-tuple-element.40), channel_id=1, source_target_pairs={{0,1},{1,0},{2,3},{3,2},{4,5},{5,4},{6,7},{7,6},{8,9},{9,8},{10,11... | collective-permute-start | bytes 32264 | tf_op jit(solution)/shard_map/ppermute | solution.py:71
  24.3 3.7 %collective-permute-start.7 = (bf16[6,896]{1,0:T(8,128)(2,1)S(1)}, bf16[6,896]{1,0:T(8,128)(2,1)S(1)}, u32[]{:S(2)}, u32[]{:S(2)}) collective-permute-start(bf16[6,896]{1,0:T(8,128)(2,1)S(1)} %get-tuple-element.41), channel_id=1, source_target_pairs={{0,2},{1,3},{2,0},{3,1},{4,6},{5,7},{6,4},{7,5},{8,10},{9,11},{10,... | collective-permute-start | bytes 32264 | tf_op jit(solution)/shard_map/ppermute | solution.py:71
  25.7 3.1 %collective-permute-start.8 = (bf16[6,896]{1,0:T(8,128)(2,1)S(1)}, bf16[6,896]{1,0:T(8,128)(2,1)S(1)}, u32[]{:S(2)}, u32[]{:S(2)}) collective-permute-start(bf16[6,896]{1,0:T(8,128)(2,1)S(1)} %get-tuple-element.42), channel_id=1, source_target_pairs={{0,3},{1,2},{2,1},{3,0},{4,7},{5,6},{6,5},{7,4},{8,11},{9,10},{10,... | collective-permute-start | bytes 32264 | tf_op jit(solution)/shard_map/ppermute | solution.py:71
  28.9 1.6 %copy-start.3 = (f32[1536]{0:T(1024)S(1)}, f32[1536]{0:T(1024)}, u32[]{:S(2)}) copy-start(f32[1536]{0:T(1024)} %param.19) | copy-start | bytes 18436
  29.7 4.1 %collective-permute-start.10 = (bf16[12,1536]{1,0:T(8,128)(2,1)S(1)}, bf16[12,1536]{1,0:T(8,128)(2,1)S(1)}, u32[]{:S(2)}, u32[]{:S(2)}) collective-permute-start(bf16[12,1536]{1,0:T(8,128)(2,1)S(1)} %out.1.refs_0_), channel_id=1, source_target_pairs={{0,2},{1,3},{2,0},{3,1},{4,6},{5,7},{6,4},{7,5},{8,10},{9,11},{10,... | collective-permute-start | bytes 110600 | tf_op jit(solution)/shard_map/ppermute | solution.py:98
  30.5 3.3 %copy-start.2 = (bf16[1536,8]{0,1:T(8,128)(2,1)S(1)}, bf16[1536,8]{0,1:T(8,128)(2,1)}, u32[]{:S(2)}) copy-start(bf16[1536,8]{0,1:T(8,128)(2,1)} %param.20) | copy-start | bytes 73732
  36.6 10.4 %all-to-all-start.1 = ((bf16[32,2,768]{2,1,0:T(2,128)(2,1)}), bf16[32,2,768]{2,1,0:T(2,128)(2,1)S(1)}, u32[]{:S(2)}, u32[]{:S(2)}) async-start(bf16[32,2,768]{2,1,0:T(2,128)(2,1)} %get-tuple-element.53), calls=%async_computation.1 | async-start | bytes 196608 | tf_op jit(solution)/shard_map/all_to_all | solution.py:644
  39.1 2.0 %collective-permute-start.11 = (bf16[2,1536]{1,0:T(2,128)(2,1)S(1)}, bf16[2,1536]{1,0:T(2,128)(2,1)S(1)}, u32[]{:S(2)}, u32[]{:S(2)}) collective-permute-start(bf16[2,1536]{1,0:T(2,128)(2,1)S(1)} %get-tuple-element.50), channel_id=1, source_target_pairs={{0,1},{1,0},{2,3},{3,2},{4,5},{5,4},{6,7},{7,6},{8,9},{9,8},{10,11... | collective-permute-start | bytes 18440 | tf_op jit(solution)/shard_map/ppermute | solution.py:71
  39.3 3.6 %collective-permute-start.12 = (bf16[2,1536]{1,0:T(2,128)(2,1)S(1)}, bf16[2,1536]{1,0:T(2,128)(2,1)S(1)}, u32[]{:S(2)}, u32[]{:S(2)}) collective-permute-start(bf16[2,1536]{1,0:T(2,128)(2,1)S(1)} %get-tuple-element.51), channel_id=1, source_target_pairs={{0,2},{1,3},{2,0},{3,1},{4,6},{5,7},{6,4},{7,5},{8,10},{9,11},{10,... | collective-permute-start | bytes 18440 | tf_op jit(solution)/shard_map/ppermute | solution.py:71
  41.0 3.1 %collective-permute-start.13 = (bf16[2,1536]{1,0:T(2,128)(2,1)S(1)}, bf16[2,1536]{1,0:T(2,128)(2,1)S(1)}, u32[]{:S(2)}, u32[]{:S(2)}) collective-permute-start(bf16[2,1536]{1,0:T(2,128)(2,1)S(1)} %get-tuple-element.52), channel_id=1, source_target_pairs={{0,3},{1,2},{2,1},{3,0},{4,7},{5,6},{6,5},{7,4},{8,11},{9,10},{10,... | collective-permute-start | bytes 18440 | tf_op jit(solution)/shard_map/ppermute | solution.py:71
where the time goes:
time: 48.1 us; the launch traced here: 47.7 us
  starting transfers between devices  18.6 us (39%)
  Pallas kernels  14.8 us (31%)
  waiting for transfers between devices  12.2 us (25%)
  between operations  1.42 us (3%)
  local copies, waits for them, and re-layouts  0.73 us (2%)
    ppermute x12, starting transfers between devices, exchanged(): arrived.append(lax.ppermute(block, 'tensor', pairs))  7.71 us
    all_to_all x1, starting transfers between devices, shards(): came = lax.all_to_all(offers, ('replica', 'tensor'), 0, 0, tiled=True)  7.3 us
    pallas_call x4, Pallas kernels, loaded(): pl.pallas_call(functools.partial(load_kernel, tuple(plans)), out_shape=sh...  7.3 us
    ppermute x12, waiting for transfers between devices, exchanged(): arrived.append(lax.ppermute(block, 'tensor', pairs))  5.49 us
    all_to_all x1, waiting for transfers between devices, shards(): guests = lax.all_to_all(guests, ('replica', 'tensor'), 0, 0, tiled=True)  2.87 us
    all_to_all x1, waiting for transfers between devices, shards(): came = lax.all_to_all(offers, ('replica', 'tensor'), 0, 0, tiled=True)  2.77 us
    pallas_call x1, Pallas kernels, shards(): pl.pallas_call(functools.partial(expert_kernel, size, top, router.shape[1...  2.74 us
    all_to_all x1, starting transfers between devices, shards(): guests = lax.all_to_all(guests, ('replica', 'tensor'), 0, 0, tiled=True)  2.57 us
  transfers between devices with their start and end apart: 16, of which 9 were waited for; matrix products, arithmetic and copies ran while one was open for 1% of the time, Pallas kernels for 17%

commit v1 on v0

--- a/solution.py
+++ b/solution.py
@@ -549,7 +549,7 @@
     offers, homes, plan, tail = pl.pallas_call(
         offer_kernel,
         out_shape=[
-            shape((everyone, 2, (wide + LANES) // 2), jnp.bfloat16),
+            pltpu.VMEM((everyone, 2, (wide + LANES) // 2), jnp.bfloat16),
             shape((home_dev, wide), jnp.bfloat16),
             shape((npages, LANES)),
             shape((1, LANES)),
@@ -592,7 +592,7 @@
     joined = exchanged(projected)
 
     before = load_more(rows, (0, 2), (0, 2))
-    late, _ = lax.optimization_barrier((out_weight, rows))
+    late, _ = lax.optimization_barrier((out_weight, joined[1]))
     out_mate = lax.ppermute(late, "tensor", [(me, me ^ 1) for me in range(size)])
     terms = pl.pallas_call(
         functools.partial(attend_kernel, size, top),
@@ -625,7 +625,7 @@
             expert_kernel, size, top, router.shape[1], len(gate_up), len(down)
         ),
         out_shape=[shape((home_dev, width), jnp.bfloat16)] * size
-        + [shape((everyone, 2, width // 2), jnp.bfloat16)],
+        + [pltpu.VMEM((everyone, 2, width // 2), jnp.bfloat16)],
         in_specs=[VMEM] * (len(sums) + 3 + len(gate_up) + len(down)),
         out_specs=[VMEM] * (size + 1),
         scratch_shapes=[

time: 48.1 us -> 48.9 us (1.017)
    ppermute x12, waiting for transfers between devices: 5.49 us -> 6.06 us  [exchanged(): arrived.append(lax.ppermute(block, 'tensor', pairs))]
  transfers between devices with their start and end apart: 16 -> 16, of which waited for: 9 -> 10; matrix products, arithmetic and copies ran while one was open for 1% -> 1% of each run, Pallas kernels for 17% -> 17%
where the time goes in v1:
time: 48.9 us; the launch traced here: 48.5 us
  starting transfers between devices  18.9 us (39%)
  Pallas kernels  14.9 us (30%)
  waiting for transfers between devices  12.4 us (25%)
  between operations  1.42 us (3%)
  local copies, waits for them, and re-layouts  0.86 us (2%)
    ppermute x12, starting transfers between devices, exchanged(): arrived.append(lax.ppermute(block, 'tensor', pairs))  7.76 us
    pallas_call x4, Pallas kernels, loaded(): pl.pallas_call(functools.partial(load_kernel, tuple(plans)), out_shape=sh...  7.38 us
    all_to_all x1, starting transfers between devices, shards(): came = lax.all_to_all(offers, ('replica', 'tensor'), 0, 0, tiled=True)  7.3 us
    ppermute x12, waiting for transfers between devices, exchanged(): arrived.append(lax.ppermute(block, 'tensor', pairs))  6.06 us
    all_to_all x1, waiting for transfers between devices, shards(): guests = lax.all_to_all(guests, ('replica', 'tensor'), 0, 0, tiled=True)  2.87 us
    all_to_all x1, waiting for transfers between devices, shards(): came = lax.all_to_all(offers, ('replica', 'tensor'), 0, 0, tiled=True)  2.77 us
    pallas_call x1, Pallas kernels, shards(): pl.pallas_call(functools.partial(expert_kernel, size, top, router.shape[1...  2.74 us
    all_to_all x1, starting transfers between devices, shards(): guests = lax.all_to_all(guests, ('replica', 'tensor'), 0, 0, tiled=True)  2.57 us
  transfers between devices with their start and end apart: 16, of which 10 were waited for; matrix products, arithmetic and copies ran while one was open for 1% of the time, Pallas kernels for 17%

profile of v1, /device:TPU:0, one launch (start us, length us, event | category | flops | bytes accessed | tf_op | source)
XLA Modules:
  0.0 48.5 jit_solution(15416992834283197212)
XLA Ops:
  1.3 1.6 %offer.1 = (bf16[32,2,896]{2,1,0:T(2,128)(2,1)}, bf16[2,1664]{1,0:T(2,128)(2,1)S(1)}, f32[6,128]{1,0:T(8,128)S(1)}, f32[1,128]{1,0:T(1,128)S(1)}) custom-call(bf16[3,1536]{1,0:T(4,128)(2,1)} %tokens.1, s32[6,12]{1,0:T(8,128)} %bitcast.12, s32[1,2]{1,0:T(1,128)} %pages.1, s32[2,8]{1,0:T(2,128)} %bitcast.13, s32[8]{0:T(128)} %lens.1, s32[1]{0:T(128)S(6)} %add.3.packed), custom_call_target="tpu_custom_call" | custom-call | tf_op jit(solution)/shard_map/offer/pallas_call | solution.py:549
  2.9 7.3 %all-to-all-start = ((bf16[32,2,896]{2,1,0:T(2,128)(2,1)}), bf16[32,2,896]{2,1,0:T(2,128)(2,1)S(1)}, u32[]{:S(2)}, u32[]{:S(2)}) async-start(bf16[32,2,896]{2,1,0:T(2,128)(2,1)} %get-tuple-element.31), calls=%async_computation | async-start | bytes 229376 | tf_op jit(solution)/shard_map/all_to_all | solution.py:570
  10.2 1.6 %collective-permute-start.2 = (bf16[2,1664]{1,0:T(2,128)(2,1)S(1)}, bf16[2,1664]{1,0:T(2,128)(2,1)S(1)}, u32[]{:S(2)}, u32[]{:S(2)}) collective-permute-start(bf16[2,1664]{1,0:T(2,128)(2,1)S(1)} %get-tuple-element.30.refs_0_), channel_id=1, source_target_pairs={{0,3},{1,2},{2,1},{3,0},{4,7},{5,6},{6,5},{7,4},{8,11},{9,10},{10,... | collective-permute-start | bytes 19976 | tf_op jit(solution)/shard_map/ppermute | solution.py:71
  11.8 0.4 collective-permute-start.1
  12.1 0.0 collective-permute-start
  12.2 0.7 %reshape.15.refs_5_ = f32[1,1536]{1,0:T(1,128)S(1)} reshape(f32[1536]{0:T(1024)} %param.16) | data formatting | bytes 12288 | tf_op jit(solution)/shard_map/reshape | solution.py:588
  12.9 1.5 %load.4.refs_6_ = bf16[1536,640]{1,0:T(8,128)(2,1)S(1)} custom-call(bf16[2,1664]{1,0:T(2,128)(2,1)S(1)} %get-tuple-element.30.refs_0_, bf16[1536,640]{1,0:T(8,128)(2,1)} %refs_1_.4), custom_call_target="tpu_custom_call" | custom-call | bytes 1966080 | tf_op jit(solution)/shard_map/load/pallas_call | solution.py:195
  14.4 0.0 copy-start.1
  14.4 0.0 collective-permute-done.2.refs_3_
  14.4 1.0 %collective-permute-done.1.refs_2_ = bf16[2,1664]{1,0:T(2,128)(2,1)S(1)} collective-permute-done((bf16[2,1664]{1,0:T(2,128)(2,1)S(1)}, bf16[2,1664]{1,0:T(2,128)(2,1)S(1)}, u32[]{:S(2)}, u32[]{:S(2)}) %collective-permute-start.1) | collective-permute-done | bytes 6688 | tf_op jit(solution)/shard_map/ppermute | solution.py:71
  15.4 0.0 collective-permute-done.refs_1_
  15.4 2.8 %all-to-all-done.refs_4_ = bf16[32,2,896]{2,1,0:T(2,128)(2,1)S(1)} async-done(((bf16[32,2,896]{2,1,0:T(2,128)(2,1)}), bf16[32,2,896]{2,1,0:T(2,128)(2,1)S(1)}, u32[]{:S(2)}, u32[]{:S(2)}) %all-to-all-start) | async-done | bytes 114720 | tf_op jit(solution)/shard_map/all_to_all | solution.py:570
  18.2 0.8 %project.1 = (f32[12,1664]{1,0:T(8,128)S(1)}, bf16[6,640]{1,0:T(8,128)(2,1)S(1)}, bf16[6,640]{1,0:T(8,128)(2,1)S(1)}, bf16[6,640]{1,0:T(8,128)(2,1)S(1)}, bf16[6,640]{1,0:T(8,128)(2,1)S(1)}) custom-call(bf16[2,1664]{1,0:T(2,128)(2,1)S(1)} %get-tuple-element.30.refs_0_, bf16[2,1664]{1,0:T(2,128)(2,1)S(1)} %collective-permute-done.refs_1_, ...), custom_call_target="tpu_custom_call" | custom-call | tf_op jit(solution)/shard_map/project/pallas_call | solution.py:574
  19.0 0.2 collective-permute-start.3
  19.2 1.0 %collective-permute-done.3.refs_1_ = bf16[6,640]{1,0:T(8,128)(2,1)S(1)} collective-permute-done((bf16[6,640]{1,0:T(8,128)(2,1)S(1)}, bf16[6,640]{1,0:T(8,128)(2,1)S(1)}, u32[]{:S(2)}, u32[]{:S(2)}) %collective-permute-start.3) | collective-permute-done | bytes 7712 | tf_op jit(solution)/shard_map/ppermute | solution.py:71
  20.2 0.0 copy-done.1
  20.2 0.2 collective-permute-start.9
  20.4 0.4 collective-permute-start.4
  20.8 1.3 %collective-permute-start.5 = (bf16[6,640]{1,0:T(8,128)(2,1)S(1)}, bf16[6,640]{1,0:T(8,128)(2,1)S(1)}, u32[]{:S(2)}, u32[]{:S(2)}) collective-permute-start(bf16[6,640]{1,0:T(8,128)(2,1)S(1)} %get-tuple-element.36), channel_id=1, source_target_pairs={{0,3},{1,2},{2,1},{3,0},{4,7},{5,6},{6,5},{7,4},{8,11},{9,10},{10,... | collective-permute-start | bytes 23048 | tf_op jit(solution)/shard_map/ppermute | solution.py:71
  22.1 1.8 %load.5 = (bf16[2,1536,2,128]{3,2,1,0:T(2,128)(2,1)S(1)}, bf16[256,1536]{1,0:T(8,128)(2,1)S(1)}) custom-call(f32[12,1664]{1,0:T(8,128)S(1)} %get-tuple-element.37.refs_0_.refs_5_.refs_2_, bf16[1536,2,1024]{2,1,0:T(2,128)(2,1)} %refs_1_.7, bf16[1024,1536]{1,0:T(8,128)(2,1)} %refs_2_.5), custom_call_target="tpu_custom_call" | custom-call | bytes 2359296 | tf_op jit(solution)/shard_map/load/pallas_call | solution.py:195
  23.9 0.2 collective-permute-done.4.refs_2_
  24.1 0.0 collective-permute-done.5.refs_3_
  24.1 0.1 copy-done
  24.2 0.7 %attend.1 = (bf16[6,896]{1,0:T(8,128)(2,1)S(1)}, bf16[6,896]{1,0:T(8,128)(2,1)S(1)}, bf16[6,896]{1,0:T(8,128)(2,1)S(1)}, bf16[6,896]{1,0:T(8,128)(2,1)S(1)}) custom-call(bf16[6,640]{1,0:T(8,128)(2,1)S(1)} %get-tuple-element.33.refs_0_, bf16[6,640]{1,0:T(8,128)(2,1)S(1)} %collective-permute-done.3.refs_1_, bf16[6,640]{1,0:T(8,128)(2,1)S(1)} %collective-permute-done.4.refs_2_, ...), custom_call_target="tpu_custom_call" | custom-call | tf_op jit(solution)/shard_map/attend/pallas_call | solution.py:597
  25.0 0.5 %collective-permute-start.6 = (bf16[6,896]{1,0:T(8,128)(2,1)S(1)}, bf16[6,896]{1,0:T(8,128)(2,1)S(1)}, u32[]{:S(2)}, u32[]{:S(2)}) collective-permute-start(bf16[6,896]{1,0:T(8,128)(2,1)S(1)} %get-tuple-element.40), channel_id=1, source_target_pairs={{0,1},{1,0},{2,3},{3,2},{4,5},{5,4},{6,7},{7,6},{8,9},{9,8},{10,11... | collective-permute-start | bytes 32264 | tf_op jit(solution)/shard_map/ppermute | solution.py:71
  25.5 1.0 %collective-permute-start.7 = (bf16[6,896]{1,0:T(8,128)(2,1)S(1)}, bf16[6,896]{1,0:T(8,128)(2,1)S(1)}, u32[]{:S(2)}, u32[]{:S(2)}) collective-permute-start(bf16[6,896]{1,0:T(8,128)(2,1)S(1)} %get-tuple-element.41), channel_id=1, source_target_pairs={{0,2},{1,3},{2,0},{3,1},{4,6},{5,7},{6,4},{7,5},{8,10},{9,11},{10,... | collective-permute-start | bytes 32264 | tf_op jit(solution)/shard_map/ppermute | solution.py:71
  26.5 0.4 collective-permute-start.8
  26.9 1.9 %load.6 = (bf16[3,1536,2,128]{3,2,1,0:T(2,128)(2,1)S(1)}, bf16[256,1536]{1,0:T(8,128)(2,1)S(1)}) custom-call(bf16[6,896]{1,0:T(8,128)(2,1)S(1)} %get-tuple-element.39.refs_0_, bf16[1536,2,1024]{2,1,0:T(2,128)(2,1)} %refs_1_.7, bf16[1024,1536]{1,0:T(8,128)(2,1)} %refs_2_.5), custom_call_target="tpu_custom_call" | custom-call | bytes 3145728 | tf_op jit(solution)/shard_map/load/pallas_call | solution.py:195
  28.8 0.0 collective-permute-done.6.refs_1_
  28.8 0.4 collective-permute-done.7.refs_2_
  29.2 0.4 collective-permute-done.8.refs_3_
  29.6 0.0 collective-permute-done.9.refs_5_
  29.6 0.8 %out.1.refs_0_ = bf16[12,1536]{1,0:T(8,128)(2,1)S(1)} custom-call(bf16[6,896]{1,0:T(8,128)(2,1)S(1)} %get-tuple-element.39.refs_0_, bf16[6,896]{1,0:T(8,128)(2,1)S(1)} %collective-permute-done.6.refs_1_, bf16[6,896]{1,0:T(8,128)(2,1)S(1)} %collective-permute-done.7.refs_2_, bf16[6,896]{1,0:T(8,128)(2,1)S(1)} %collective-permute-done.8.refs_3_, ...), custom_call_target="tpu_custom_call" | custom-call | tf_op jit(solution)/shard_map/out/pallas_call | solution.py:612
  30.5 1.1 %collective-permute-start.10 = (bf16[12,1536]{1,0:T(8,128)(2,1)S(1)}, bf16[12,1536]{1,0:T(8,128)(2,1)S(1)}, u32[]{:S(2)}, u32[]{:S(2)}) collective-permute-start(bf16[12,1536]{1,0:T(8,128)(2,1)S(1)} %out.1.refs_0_), channel_id=1, source_target_pairs={{0,2},{1,3},{2,0},{3,1},{4,6},{5,7},{6,4},{7,5},{8,10},{9,11},{10,... | collective-permute-start | bytes 110600 | tf_op jit(solution)/shard_map/ppermute | solution.py:98
  31.6 0.0 copy-done.3
  31.6 0.0 copy-start.2
  31.7 2.2 %load.7 = (bf16[3,1536,2,128]{3,2,1,0:T(2,128)(2,1)S(1)}, bf16[512,1536]{1,0:T(8,128)(2,1)S(1)}) custom-call(bf16[12,1536]{1,0:T(8,128)(2,1)S(1)} %out.1.refs_0_, bf16[1536,2,1024]{2,1,0:T(2,128)(2,1)} %refs_1_.7, bf16[1024,1536]{1,0:T(8,128)(2,1)} %refs_2_.5), custom_call_target="tpu_custom_call" | custom-call | bytes 3932160 | tf_op jit(solution)/shard_map/load/pallas_call | solution.py:195
  33.9 0.7 %collective-permute-done.10.refs_1_ = bf16[12,1536]{1,0:T(8,128)(2,1)S(1)} collective-permute-done((bf16[12,1536]{1,0:T(8,128)(2,1)S(1)}, bf16[12,1536]{1,0:T(8,128)(2,1)S(1)}, u32[]{:S(2)}, u32[]{:S(2)}) %collective-permute-start.10) | collective-permute-done | bytes 36896 | tf_op jit(solution)/shard_map/ppermute | solution.py:98
  34.6 2.7 %experts.1 = (bf16[2,1536]{1,0:T(2,128)(2,1)S(1)}, bf16[2,1536]{1,0:T(2,128)(2,1)S(1)}, bf16[2,1536]{1,0:T(2,128)(2,1)S(1)}, bf16[2,1536]{1,0:T(2,128)(2,1)S(1)}, bf16[32,2,768]{2,1,0:T(2,128)(2,1)}) custom-call(bf16[12,1536]{1,0:T(8,128)(2,1)S(1)} %out.1.refs_0_, bf16[12,1536]{1,0:T(8,128)(2,1)S(1)} %collective-permute-done.10.refs_1_, ...), custom_call_target="tpu_custom_call" | custom-call | tf_op jit(solution)/shard_map/experts/pallas_call | solution.py:623
  37.3 2.6 %all-to-all-start.1 = ((bf16[32,2,768]{2,1,0:T(2,128)(2,1)}), bf16[32,2,768]{2,1,0:T(2,128)(2,1)S(1)}, u32[]{:S(2)}, u32[]{:S(2)}) async-start(bf16[32,2,768]{2,1,0:T(2,128)(2,1)} %get-tuple-element.53), calls=%async_computation.1 | async-start | bytes 196608 | tf_op jit(solution)/shard_map/all_to_all | solution.py:644
  39.9 0.2 collective-permute-start.11
  40.1 1.7 %collective-permute-start.12 = (bf16[2,1536]{1,0:T(2,128)(2,1)S(1)}, bf16[2,1536]{1,0:T(2,128)(2,1)S(1)}, u32[]{:S(2)}, u32[]{:S(2)}) collective-permute-start(bf16[2,1536]{1,0:T(2,128)(2,1)S(1)} %get-tuple-element.51), channel_id=1, source_target_pairs={{0,2},{1,3},{2,0},{3,1},{4,6},{5,7},{6,4},{7,5},{8,10},{9,11},{10,... | collective-permute-start | bytes 18440 | tf_op jit(solution)/shard_map/ppermute | solution.py:71
  41.8 0.1 collective-permute-start.13
  41.9 0.0 collective-permute-done.11.refs_1_
  41.9 1.9 %collective-permute-done.12.refs_2_ = bf16[2,1536]{1,0:T(2,128)(2,1)S(1)} collective-permute-done((bf16[2,1536]{1,0:T(2,128)(2,1)S(1)}, bf16[2,1536]{1,0:T(2,128)(2,1)S(1)}, u32[]{:S(2)}, u32[]{:S(2)}) %collective-permute-start.12) | collective-permute-done | bytes 6176 | tf_op jit(solution)/shard_map/ppermute | solution.py:71
  43.7 1.1 %collective-permute-done.13.refs_3_ = bf16[2,1536]{1,0:T(2,128)(2,1)S(1)} collective-permute-done((bf16[2,1536]{1,0:T(2,128)(2,1)S(1)}, bf16[2,1536]{1,0:T(2,128)(2,1)S(1)}, u32[]{:S(2)}, u32[]{:S(2)}) %collective-permute-start.13) | collective-permute-done | bytes 6176 | tf_op jit(solution)/shard_map/ppermute | solution.py:71
  44.8 2.9 %all-to-all-done.1.refs_4_ = bf16[32,2,768]{2,1,0:T(2,128)(2,1)S(1)} async-done(((bf16[32,2,768]{2,1,0:T(2,128)(2,1)}), bf16[32,2,768]{2,1,0:T(2,128)(2,1)S(1)}, u32[]{:S(2)}, u32[]{:S(2)}) %all-to-all-start.1) | async-done | bytes 98336 | tf_op jit(solution)/shard_map/all_to_all | solution.py:644
  47.7 0.8 %finish.1 = bf16[3,1536]{1,0:T(4,128)(2,1)} custom-call(bf16[2,1536]{1,0:T(2,128)(2,1)S(1)} %get-tuple-element.49.refs_0_, bf16[2,1536]{1,0:T(2,128)(2,1)S(1)} %collective-permute-done.11.refs_1_, bf16[2,1536]{1,0:T(2,128)(2,1)S(1)} %collective-permute-done.12.refs_2_, bf16[2,1536]{1,0:T(2,128)(2,1)S(1)} %collective-permute-done.13.refs_3_, ...), custom_call_target="tpu_custom_call" | custom-call | tf_op jit(solution)/shard_map/finish/pallas_call | solution.py:646
  (4 shorter events, 0.0 us)
Async XLA Ops:
  2.9 15.3 %all-to-all-start = ((bf16[32,2,896]{2,1,0:T(2,128)(2,1)}), bf16[32,2,896]{2,1,0:T(2,128)(2,1)S(1)}, u32[]{:S(2)}, u32[]{:S(2)}) async-start(bf16[32,2,896]{2,1,0:T(2,128)(2,1)} %get-tuple-element.31), calls=%async_computation | async-start | bytes 229376 | tf_op jit(solution)/shard_map/all_to_all | solution.py:570
  10.2 4.2 %collective-permute-start.2 = (bf16[2,1664]{1,0:T(2,128)(2,1)S(1)}, bf16[2,1664]{1,0:T(2,128)(2,1)S(1)}, u32[]{:S(2)}, u32[]{:S(2)}) collective-permute-start(bf16[2,1664]{1,0:T(2,128)(2,1)S(1)} %get-tuple-element.30.refs_0_), channel_id=1, source_target_pairs={{0,3},{1,2},{2,1},{3,0},{4,7},{5,6},{6,5},{7,4},{8,11},{9,10},{10,... | collective-permute-start | bytes 19976 | tf_op jit(solution)/shard_map/ppermute | solution.py:71
  11.8 3.7 %collective-permute-start.1 = (bf16[2,1664]{1,0:T(2,128)(2,1)S(1)}, bf16[2,1664]{1,0:T(2,128)(2,1)S(1)}, u32[]{:S(2)}, u32[]{:S(2)}) collective-permute-start(bf16[2,1664]{1,0:T(2,128)(2,1)S(1)} %get-tuple-element.30.refs_0_), channel_id=1, source_target_pairs={{0,2},{1,3},{2,0},{3,1},{4,6},{5,7},{6,4},{7,5},{8,10},{9,11},{10,... | collective-permute-start | bytes 19976 | tf_op jit(solution)/shard_map/ppermute | solution.py:71
  12.1 3.3 %collective-permute-start = (bf16[2,1664]{1,0:T(2,128)(2,1)S(1)}, bf16[2,1664]{1,0:T(2,128)(2,1)S(1)}, u32[]{:S(2)}, u32[]{:S(2)}) collective-permute-start(bf16[2,1664]{1,0:T(2,128)(2,1)S(1)} %get-tuple-element.30.refs_0_), channel_id=1, source_target_pairs={{0,1},{1,0},{2,3},{3,2},{4,5},{5,4},{6,7},{7,6},{8,9},{9,8},{10,11... | collective-permute-start | bytes 19976 | tf_op jit(solution)/shard_map/ppermute | solution.py:71
  14.4 5.9 %copy-start.1 = (bf16[384,1536]{1,0:T(8,128)(2,1)S(1)}, bf16[384,1536]{1,0:T(8,128)(2,1)}, u32[]{:S(2)}) copy-start(bf16[384,1536]{1,0:T(8,128)(2,1)} %refs_4_.3) | copy-start | bytes 3538948
  19.0 1.2 %collective-permute-start.3 = (bf16[6,640]{1,0:T(8,128)(2,1)S(1)}, bf16[6,640]{1,0:T(8,128)(2,1)S(1)}, u32[]{:S(2)}, u32[]{:S(2)}) collective-permute-start(bf16[6,640]{1,0:T(8,128)(2,1)S(1)} %get-tuple-element.34), channel_id=1, source_target_pairs={{0,1},{1,0},{2,3},{3,2},{4,5},{5,4},{6,7},{7,6},{8,9},{9,8},{10,11... | collective-permute-start | bytes 23048 | tf_op jit(solution)/shard_map/ppermute | solution.py:71
  20.2 9.4 %collective-permute-start.9 = (bf16[384,1536]{1,0:T(8,128)(2,1)S(1)}, bf16[384,1536]{1,0:T(8,128)(2,1)S(1)}, u32[]{:S(2)}, u32[]{:S(2)}) collective-permute-start(bf16[384,1536]{1,0:T(8,128)(2,1)S(1)} %copy-done.1), channel_id=1, source_target_pairs={{0,1},{1,0},{2,3},{3,2},{4,5},{5,4},{6,7},{7,6},{8,9},{9,8},{10,11... | collective-permute-start | bytes 3538952 | tf_op jit(solution)/shard_map/ppermute | solution.py:596
  20.4 3.7 %collective-permute-start.4 = (bf16[6,640]{1,0:T(8,128)(2,1)S(1)}, bf16[6,640]{1,0:T(8,128)(2,1)S(1)}, u32[]{:S(2)}, u32[]{:S(2)}) collective-permute-start(bf16[6,640]{1,0:T(8,128)(2,1)S(1)} %get-tuple-element.35), channel_id=1, source_target_pairs={{0,2},{1,3},{2,0},{3,1},{4,6},{5,7},{6,4},{7,5},{8,10},{9,11},{10,... | collective-permute-start | bytes 23048 | tf_op jit(solution)/shard_map/ppermute | solution.py:71
  20.8 3.3 %collective-permute-start.5 = (bf16[6,640]{1,0:T(8,128)(2,1)S(1)}, bf16[6,640]{1,0:T(8,128)(2,1)S(1)}, u32[]{:S(2)}, u32[]{:S(2)}) collective-permute-start(bf16[6,640]{1,0:T(8,128)(2,1)S(1)} %get-tuple-element.36), channel_id=1, source_target_pairs={{0,3},{1,2},{2,1},{3,0},{4,7},{5,6},{6,5},{7,4},{8,11},{9,10},{10,... | collective-permute-start | bytes 23048 | tf_op jit(solution)/shard_map/ppermute | solution.py:71
  22.1 2.1 %copy-start = (bf16[6,2,128,512]{3,2,1,0:T(8,128)(2,1)S(1)}, bf16[6,2,128,512]{3,2,1,0:T(8,128)(2,1)}, u32[]{:S(2)}) copy-start(bf16[6,2,128,512]{3,2,1,0:T(8,128)(2,1)} %refs_4_.2) | copy-start | bytes 4718596
  25.0 3.9 %collective-permute-start.6 = (bf16[6,896]{1,0:T(8,128)(2,1)S(1)}, bf16[6,896]{1,0:T(8,128)(2,1)S(1)}, u32[]{:S(2)}, u32[]{:S(2)}) collective-permute-start(bf16[6,896]{1,0:T(8,128)(2,1)S(1)} %get-tuple-element.40), channel_id=1, source_target_pairs={{0,1},{1,0},{2,3},{3,2},{4,5},{5,4},{6,7},{7,6},{8,9},{9,8},{10,11... | collective-permute-start | bytes 32264 | tf_op jit(solution)/shard_map/ppermute | solution.py:71
  25.5 3.7 %collective-permute-start.7 = (bf16[6,896]{1,0:T(8,128)(2,1)S(1)}, bf16[6,896]{1,0:T(8,128)(2,1)S(1)}, u32[]{:S(2)}, u32[]{:S(2)}) collective-permute-start(bf16[6,896]{1,0:T(8,128)(2,1)S(1)} %get-tuple-element.41), channel_id=1, source_target_pairs={{0,2},{1,3},{2,0},{3,1},{4,6},{5,7},{6,4},{7,5},{8,10},{9,11},{10,... | collective-permute-start | bytes 32264 | tf_op jit(solution)/shard_map/ppermute | solution.py:71
  26.5 3.1 %collective-permute-start.8 = (bf16[6,896]{1,0:T(8,128)(2,1)S(1)}, bf16[6,896]{1,0:T(8,128)(2,1)S(1)}, u32[]{:S(2)}, u32[]{:S(2)}) collective-permute-start(bf16[6,896]{1,0:T(8,128)(2,1)S(1)} %get-tuple-element.42), channel_id=1, source_target_pairs={{0,3},{1,2},{2,1},{3,0},{4,7},{5,6},{6,5},{7,4},{8,11},{9,10},{10,... | collective-permute-start | bytes 32264 | tf_op jit(solution)/shard_map/ppermute | solution.py:71
  29.6 2.0 %copy-start.3 = (f32[1536]{0:T(1024)S(1)}, f32[1536]{0:T(1024)}, u32[]{:S(2)}) copy-start(f32[1536]{0:T(1024)} %param.19) | copy-start | bytes 18436
  30.5 4.1 %collective-permute-start.10 = (bf16[12,1536]{1,0:T(8,128)(2,1)S(1)}, bf16[12,1536]{1,0:T(8,128)(2,1)S(1)}, u32[]{:S(2)}, u32[]{:S(2)}) collective-permute-start(bf16[12,1536]{1,0:T(8,128)(2,1)S(1)} %out.1.refs_0_), channel_id=1, source_target_pairs={{0,2},{1,3},{2,0},{3,1},{4,6},{5,7},{6,4},{7,5},{8,10},{9,11},{10,... | collective-permute-start | bytes 110600 | tf_op jit(solution)/shard_map/ppermute | solution.py:98
  31.6 2.9 %copy-start.2 = (bf16[1536,8]{0,1:T(8,128)(2,1)S(1)}, bf16[1536,8]{0,1:T(8,128)(2,1)}, u32[]{:S(2)}) copy-start(bf16[1536,8]{0,1:T(8,128)(2,1)} %param.20) | copy-start | bytes 73732
  37.3 10.4 %all-to-all-start.1 = ((bf16[32,2,768]{2,1,0:T(2,128)(2,1)}), bf16[32,2,768]{2,1,0:T(2,128)(2,1)S(1)}, u32[]{:S(2)}, u32[]{:S(2)}) async-start(bf16[32,2,768]{2,1,0:T(2,128)(2,1)} %get-tuple-element.53), calls=%async_computation.1 | async-start | bytes 196608 | tf_op jit(solution)/shard_map/all_to_all | solution.py:644
  39.9 2.0 %collective-permute-start.11 = (bf16[2,1536]{1,0:T(2,128)(2,1)S(1)}, bf16[2,1536]{1,0:T(2,128)(2,1)S(1)}, u32[]{:S(2)}, u32[]{:S(2)}) collective-permute-start(bf16[2,1536]{1,0:T(2,128)(2,1)S(1)} %get-tuple-element.50), channel_id=1, source_target_pairs={{0,1},{1,0},{2,3},{3,2},{4,5},{5,4},{6,7},{7,6},{8,9},{9,8},{10,11... | collective-permute-start | bytes 18440 | tf_op jit(solution)/shard_map/ppermute | solution.py:71
  40.1 3.6 %collective-permute-start.12 = (bf16[2,1536]{1,0:T(2,128)(2,1)S(1)}, bf16[2,1536]{1,0:T(2,128)(2,1)S(1)}, u32[]{:S(2)}, u32[]{:S(2)}) collective-permute-start(bf16[2,1536]{1,0:T(2,128)(2,1)S(1)} %get-tuple-element.51), channel_id=1, source_target_pairs={{0,2},{1,3},{2,0},{3,1},{4,6},{5,7},{6,4},{7,5},{8,10},{9,11},{10,... | collective-permute-start | bytes 18440 | tf_op jit(solution)/shard_map/ppermute | solution.py:71
  41.8 3.1 %collective-permute-start.13 = (bf16[2,1536]{1,0:T(2,128)(2,1)S(1)}, bf16[2,1536]{1,0:T(2,128)(2,1)S(1)}, u32[]{:S(2)}, u32[]{:S(2)}) collective-permute-start(bf16[2,1536]{1,0:T(2,128)(2,1)S(1)} %get-tuple-element.52), channel_id=1, source_target_pairs={{0,3},{1,2},{2,1},{3,0},{4,7},{5,6},{6,5},{7,4},{8,11},{9,10},{10,... | collective-permute-start | bytes 18440 | tf_op jit(solution)/shard_map/ppermute | solution.py:71

commit v2 on v0

--- a/solution.py
+++ b/solution.py
@@ -445,10 +445,12 @@
         lines = slice(b * padded, (b + 1) * padded)
         left.append(jnp.concatenate([to_gate[lines], to_up[lines]], axis=0))
     left = jnp.concatenate(left, axis=1)
-    both = []
+    both, right = [], []
     for piece in gate_up:
-        right = jnp.concatenate([piece[place] for place in range(piece.shape[0])], axis=1)
-        both.append(jnp.dot(left, right, preferred_element_type=jnp.float32))
+        right += [piece[place] for place in range(piece.shape[0])]
+    for place in range(0, len(right), 2):
+        pair = jnp.concatenate(right[place : place + 2], axis=1)
+        both.append(jnp.dot(left, pair, preferred_element_type=jnp.float32))
     both = jnp.concatenate(both, axis=1)
     gate, up = both[:count], both[padded : padded + count]
     activated = gate / (1.0 + jnp.exp(-gate)) * up
@@ -591,7 +593,7 @@
     )
     joined = exchanged(projected)
 
-    before = load_more(rows, (0, 2), (0, 2))
+    before = load_more(rows, (0, 2), (0, 4))
     late, _ = lax.optimization_barrier((out_weight, rows))
     out_mate = lax.ppermute(late, "tensor", [(me, me ^ 1) for me in range(size)])
     terms = pl.pallas_call(
@@ -608,7 +610,7 @@
     )(*joined, resident(kv_cache), rows, plan, before)
     arrived = exchanged(terms)
 
-    before = load_more(terms[0], (2, 5), (2, 4))
+    before = load_more(terms[0], (2, 5), (4, 6))
     partial = pl.pallas_call(
         functools.partial(out_kernel, size, npages),
         out_shape=shape((count, width), jnp.bfloat16),
@@ -619,7 +621,7 @@
     )(*arrived, resident(out_weight), resident(out_mate), plan, before)
     sums = across(partial, size)
 
-    load_more(partial, (5, 8), (4, 8))
+    load_more(partial, (5, 8), (6, 8))
     *pieces, guests = pl.pallas_call(
         functools.partial(
             expert_kernel, size, top, router.shape[1], len(gate_up), len(down)

time: 48.1 us -> 48 us (level)
  no operation moved by 1% of the time
where the time goes in v2:
time: 48 us; the launch traced here: 47.6 us
  starting transfers between devices  18.8 us (39%)
  Pallas kernels  14.7 us (31%)
  waiting for transfers between devices  12.1 us (25%)
  between operations  1.42 us (3%)
  local copies, waits for them, and re-layouts  0.73 us (2%)
    ppermute x12, starting transfers between devices, exchanged(): arrived.append(lax.ppermute(block, 'tensor', pairs))  7.71 us
    all_to_all x1, starting transfers between devices, shards(): came = lax.all_to_all(offers, ('replica', 'tensor'), 0, 0, tiled=True)  7.3 us
    pallas_call x4, Pallas kernels, loaded(): pl.pallas_call(functools.partial(load_kernel, tuple(plans)), out_shape=sh...  7.25 us
    ppermute x12, waiting for transfers between devices, exchanged(): arrived.append(lax.ppermute(block, 'tensor', pairs))  5.28 us
    all_to_all x1, waiting for transfers between devices, shards(): guests = lax.all_to_all(guests, ('replica', 'tensor'), 0, 0, tiled=True)  2.87 us
    all_to_all x1, waiting for transfers between devices, shards(): came = lax.all_to_all(offers, ('replica', 'tensor'), 0, 0, tiled=True)  2.77 us
    pallas_call x1, Pallas kernels, shards(): pl.pallas_call(functools.partial(expert_kernel, size, top, router.shape[1...  2.64 us
    all_to_all x1, starting transfers between devices, shards(): guests = lax.all_to_all(guests, ('replica', 'tensor'), 0, 0, tiled=True)  2.57 us
  transfers between devices with their start and end apart: 16, of which 9 were waited for; matrix products, arithmetic and copies ran while one was open for 1% of the time, Pallas kernels for 17%

profile of v2, /device:TPU:0, one launch (start us, length us, event | category | flops | bytes accessed | tf_op | source)
XLA Modules:
  0.0 47.6 jit_solution(16767935201615464863)
XLA Ops:
  1.3 1.6 %offer.1 = (bf16[32,2,896]{2,1,0:T(2,128)(2,1)}, bf16[2,1664]{1,0:T(2,128)(2,1)S(1)}, f32[6,128]{1,0:T(8,128)S(1)}, f32[1,128]{1,0:T(1,128)S(1)}) custom-call(bf16[3,1536]{1,0:T(4,128)(2,1)} %tokens.1, s32[6,12]{1,0:T(8,128)} %bitcast.12, s32[1,2]{1,0:T(1,128)} %pages.1, s32[2,8]{1,0:T(2,128)} %bitcast.13, s32[8]{0:T(128)} %lens.1, s32[1]{0:T(128)S(6)} %add.3.packed), custom_call_target="tpu_custom_call" | custom-call | tf_op jit(solution)/shard_map/offer/pallas_call | solution.py:551
  2.9 7.3 %all-to-all-start = ((bf16[32,2,896]{2,1,0:T(2,128)(2,1)}), bf16[32,2,896]{2,1,0:T(2,128)(2,1)S(1)}, u32[]{:S(2)}, u32[]{:S(2)}) async-start(bf16[32,2,896]{2,1,0:T(2,128)(2,1)} %get-tuple-element.31), calls=%async_computation | async-start | bytes 229376 | tf_op jit(solution)/shard_map/all_to_all | solution.py:572
  10.2 1.6 %collective-permute-start.2 = (bf16[2,1664]{1,0:T(2,128)(2,1)S(1)}, bf16[2,1664]{1,0:T(2,128)(2,1)S(1)}, u32[]{:S(2)}, u32[]{:S(2)}) collective-permute-start(bf16[2,1664]{1,0:T(2,128)(2,1)S(1)} %get-tuple-element.30.refs_0_), channel_id=1, source_target_pairs={{0,3},{1,2},{2,1},{3,0},{4,7},{5,6},{6,5},{7,4},{8,11},{9,10},{10,... | collective-permute-start | bytes 19976 | tf_op jit(solution)/shard_map/ppermute | solution.py:71
  11.8 0.4 collective-permute-start.1
  12.1 0.0 collective-permute-start
  12.2 0.7 %reshape.15.refs_5_ = f32[1,1536]{1,0:T(1,128)S(1)} reshape(f32[1536]{0:T(1024)} %param.16) | data formatting | bytes 12288 | tf_op jit(solution)/shard_map/reshape | solution.py:590
  12.9 1.5 %load.4.refs_6_ = bf16[1536,640]{1,0:T(8,128)(2,1)S(1)} custom-call(bf16[2,1664]{1,0:T(2,128)(2,1)S(1)} %get-tuple-element.30.refs_0_, bf16[1536,640]{1,0:T(8,128)(2,1)} %refs_1_.4), custom_call_target="tpu_custom_call" | custom-call | bytes 1966080 | tf_op jit(solution)/shard_map/load/pallas_call | solution.py:195
  14.4 0.0 copy-start.1
  14.4 0.0 collective-permute-done.2.refs_3_
  14.4 1.0 %collective-permute-done.1.refs_2_ = bf16[2,1664]{1,0:T(2,128)(2,1)S(1)} collective-permute-done((bf16[2,1664]{1,0:T(2,128)(2,1)S(1)}, bf16[2,1664]{1,0:T(2,128)(2,1)S(1)}, u32[]{:S(2)}, u32[]{:S(2)}) %collective-permute-start.1) | collective-permute-done | bytes 6688 | tf_op jit(solution)/shard_map/ppermute | solution.py:71
  15.4 0.0 collective-permute-done.refs_1_
  15.4 2.8 %all-to-all-done.refs_4_ = bf16[32,2,896]{2,1,0:T(2,128)(2,1)S(1)} async-done(((bf16[32,2,896]{2,1,0:T(2,128)(2,1)}), bf16[32,2,896]{2,1,0:T(2,128)(2,1)S(1)}, u32[]{:S(2)}, u32[]{:S(2)}) %all-to-all-start) | async-done | bytes 114720 | tf_op jit(solution)/shard_map/all_to_all | solution.py:572
  18.2 0.8 %project.1 = (f32[12,1664]{1,0:T(8,128)S(1)}, bf16[6,640]{1,0:T(8,128)(2,1)S(1)}, bf16[6,640]{1,0:T(8,128)(2,1)S(1)}, bf16[6,640]{1,0:T(8,128)(2,1)S(1)}, bf16[6,640]{1,0:T(8,128)(2,1)S(1)}) custom-call(bf16[2,1664]{1,0:T(2,128)(2,1)S(1)} %get-tuple-element.30.refs_0_, bf16[2,1664]{1,0:T(2,128)(2,1)S(1)} %collective-permute-done.refs_1_, ...), custom_call_target="tpu_custom_call" | custom-call | tf_op jit(solution)/shard_map/project/pallas_call | solution.py:576
  19.0 0.0 copy-done.1
  19.0 0.2 collective-permute-start.9
  19.3 0.3 collective-permute-start.3
  19.6 0.4 collective-permute-start.4
  20.0 1.1 %collective-permute-start.5 = (bf16[6,640]{1,0:T(8,128)(2,1)S(1)}, bf16[6,640]{1,0:T(8,128)(2,1)S(1)}, u32[]{:S(2)}, u32[]{:S(2)}) collective-permute-start(bf16[6,640]{1,0:T(8,128)(2,1)S(1)} %get-tuple-element.36), channel_id=1, source_target_pairs={{0,3},{1,2},{2,1},{3,0},{4,7},{5,6},{6,5},{7,4},{8,11},{9,10},{10,... | collective-permute-start | bytes 23048 | tf_op jit(solution)/shard_map/ppermute | solution.py:71
  21.1 1.9 %load.5 = (bf16[2,1536,2,128]{3,2,1,0:T(2,128)(2,1)S(1)}, bf16[512,1536]{1,0:T(8,128)(2,1)S(1)}) custom-call(f32[12,1664]{1,0:T(8,128)S(1)} %get-tuple-element.37.refs_0_.refs_5_.refs_2_, bf16[1536,2,1024]{2,1,0:T(2,128)(2,1)} %refs_1_.7, bf16[1024,1536]{1,0:T(8,128)(2,1)} %refs_2_.5), custom_call_target="tpu_custom_call" | custom-call | bytes 3145728 | tf_op jit(solution)/shard_map/load/pallas_call | solution.py:195
  23.0 0.0 collective-permute-done.3.refs_1_
  23.0 0.2 collective-permute-done.4.refs_2_
  23.3 0.0 collective-permute-done.5.refs_3_
  23.3 0.0 copy-done
  23.3 0.7 %attend.1 = (bf16[6,896]{1,0:T(8,128)(2,1)S(1)}, bf16[6,896]{1,0:T(8,128)(2,1)S(1)}, bf16[6,896]{1,0:T(8,128)(2,1)S(1)}, bf16[6,896]{1,0:T(8,128)(2,1)S(1)}) custom-call(bf16[6,640]{1,0:T(8,128)(2,1)S(1)} %get-tuple-element.33.refs_0_, bf16[6,640]{1,0:T(8,128)(2,1)S(1)} %collective-permute-done.3.refs_1_, bf16[6,640]{1,0:T(8,128)(2,1)S(1)} %collective-permute-done.4.refs_2_, ...), custom_call_target="tpu_custom_call" | custom-call | tf_op jit(solution)/shard_map/attend/pallas_call | solution.py:599
  24.0 0.5 collective-permute-start.6
  24.5 1.2 %collective-permute-start.7 = (bf16[6,896]{1,0:T(8,128)(2,1)S(1)}, bf16[6,896]{1,0:T(8,128)(2,1)S(1)}, u32[]{:S(2)}, u32[]{:S(2)}) collective-permute-start(bf16[6,896]{1,0:T(8,128)(2,1)S(1)} %get-tuple-element.41), channel_id=1, source_target_pairs={{0,2},{1,3},{2,0},{3,1},{4,6},{5,7},{6,4},{7,5},{8,10},{9,11},{10,... | collective-permute-start | bytes 32264 | tf_op jit(solution)/shard_map/ppermute | solution.py:71
  25.7 0.2 collective-permute-start.8
  25.9 1.9 %load.6 = (bf16[3,1536,2,128]{3,2,1,0:T(2,128)(2,1)S(1)}, bf16[256,1536]{1,0:T(8,128)(2,1)S(1)}) custom-call(bf16[6,896]{1,0:T(8,128)(2,1)S(1)} %get-tuple-element.39.refs_0_, bf16[1536,2,1024]{2,1,0:T(2,128)(2,1)} %refs_1_.7, bf16[1024,1536]{1,0:T(8,128)(2,1)} %refs_2_.5), custom_call_target="tpu_custom_call" | custom-call | bytes 3145728 | tf_op jit(solution)/shard_map/load/pallas_call | solution.py:195
  27.9 0.0 collective-permute-done.6.refs_1_
  27.9 0.3 collective-permute-done.7.refs_2_
  28.2 0.7 %collective-permute-done.8.refs_3_ = bf16[6,896]{1,0:T(8,128)(2,1)S(1)} collective-permute-done((bf16[6,896]{1,0:T(8,128)(2,1)S(1)}, bf16[6,896]{1,0:T(8,128)(2,1)S(1)}, u32[]{:S(2)}, u32[]{:S(2)}) %collective-permute-start.8) | collective-permute-done | bytes 10784 | tf_op jit(solution)/shard_map/ppermute | solution.py:71
  28.9 0.0 collective-permute-done.9.refs_5_
  28.9 0.8 %out.1.refs_0_ = bf16[12,1536]{1,0:T(8,128)(2,1)S(1)} custom-call(bf16[6,896]{1,0:T(8,128)(2,1)S(1)} %get-tuple-element.39.refs_0_, bf16[6,896]{1,0:T(8,128)(2,1)S(1)} %collective-permute-done.6.refs_1_, bf16[6,896]{1,0:T(8,128)(2,1)S(1)} %collective-permute-done.7.refs_2_, bf16[6,896]{1,0:T(8,128)(2,1)S(1)} %collective-permute-done.8.refs_3_, ...), custom_call_target="tpu_custom_call" | custom-call | tf_op jit(solution)/shard_map/out/pallas_call | solution.py:614
  29.7 1.0 %collective-permute-start.10 = (bf16[12,1536]{1,0:T(8,128)(2,1)S(1)}, bf16[12,1536]{1,0:T(8,128)(2,1)S(1)}, u32[]{:S(2)}, u32[]{:S(2)}) collective-permute-start(bf16[12,1536]{1,0:T(8,128)(2,1)S(1)} %out.1.refs_0_), channel_id=1, source_target_pairs={{0,2},{1,3},{2,0},{3,1},{4,6},{5,7},{6,4},{7,5},{8,10},{9,11},{10,... | collective-permute-start | bytes 110600 | tf_op jit(solution)/shard_map/ppermute | solution.py:98
  30.7 0.0 copy-done.3
  30.7 0.0 copy-start.2
  30.7 2.0 %load.7 = (bf16[3,1536,2,128]{3,2,1,0:T(2,128)(2,1)S(1)}, bf16[256,1536]{1,0:T(8,128)(2,1)S(1)}) custom-call(bf16[12,1536]{1,0:T(8,128)(2,1)S(1)} %out.1.refs_0_, bf16[1536,2,1024]{2,1,0:T(2,128)(2,1)} %refs_1_.7, bf16[1024,1536]{1,0:T(8,128)(2,1)} %refs_2_.5), custom_call_target="tpu_custom_call" | custom-call | bytes 3145728 | tf_op jit(solution)/shard_map/load/pallas_call | solution.py:195
  32.7 1.2 %collective-permute-done.10.refs_1_ = bf16[12,1536]{1,0:T(8,128)(2,1)S(1)} collective-permute-done((bf16[12,1536]{1,0:T(8,128)(2,1)S(1)}, bf16[12,1536]{1,0:T(8,128)(2,1)S(1)}, u32[]{:S(2)}, u32[]{:S(2)}) %collective-permute-start.10) | collective-permute-done | bytes 36896 | tf_op jit(solution)/shard_map/ppermute | solution.py:98
  33.8 2.6 %experts.1 = (bf16[2,1536]{1,0:T(2,128)(2,1)S(1)}, bf16[2,1536]{1,0:T(2,128)(2,1)S(1)}, bf16[2,1536]{1,0:T(2,128)(2,1)S(1)}, bf16[2,1536]{1,0:T(2,128)(2,1)S(1)}, bf16[32,2,768]{2,1,0:T(2,128)(2,1)}) custom-call(bf16[12,1536]{1,0:T(8,128)(2,1)S(1)} %out.1.refs_0_, bf16[12,1536]{1,0:T(8,128)(2,1)S(1)} %collective-permute-done.10.refs_1_, ...), custom_call_target="tpu_custom_call" | custom-call | tf_op jit(solution)/shard_map/experts/pallas_call | solution.py:625
  36.5 2.6 %all-to-all-start.1 = ((bf16[32,2,768]{2,1,0:T(2,128)(2,1)}), bf16[32,2,768]{2,1,0:T(2,128)(2,1)S(1)}, u32[]{:S(2)}, u32[]{:S(2)}) async-start(bf16[32,2,768]{2,1,0:T(2,128)(2,1)} %get-tuple-element.53), calls=%async_computation.1 | async-start | bytes 196608 | tf_op jit(solution)/shard_map/all_to_all | solution.py:646
  39.0 0.2 collective-permute-start.11
  39.2 1.7 %collective-permute-start.12 = (bf16[2,1536]{1,0:T(2,128)(2,1)S(1)}, bf16[2,1536]{1,0:T(2,128)(2,1)S(1)}, u32[]{:S(2)}, u32[]{:S(2)}) collective-permute-start(bf16[2,1536]{1,0:T(2,128)(2,1)S(1)} %get-tuple-element.51), channel_id=1, source_target_pairs={{0,2},{1,3},{2,0},{3,1},{4,6},{5,7},{6,4},{7,5},{8,10},{9,11},{10,... | collective-permute-start | bytes 18440 | tf_op jit(solution)/shard_map/ppermute | solution.py:71
  40.9 0.1 collective-permute-start.13
  41.0 0.0 collective-permute-done.11.refs_1_
  41.0 1.9 %collective-permute-done.12.refs_2_ = bf16[2,1536]{1,0:T(2,128)(2,1)S(1)} collective-permute-done((bf16[2,1536]{1,0:T(2,128)(2,1)S(1)}, bf16[2,1536]{1,0:T(2,128)(2,1)S(1)}, u32[]{:S(2)}, u32[]{:S(2)}) %collective-permute-start.12) | collective-permute-done | bytes 6176 | tf_op jit(solution)/shard_map/ppermute | solution.py:71
  42.9 1.1 %collective-permute-done.13.refs_3_ = bf16[2,1536]{1,0:T(2,128)(2,1)S(1)} collective-permute-done((bf16[2,1536]{1,0:T(2,128)(2,1)S(1)}, bf16[2,1536]{1,0:T(2,128)(2,1)S(1)}, u32[]{:S(2)}, u32[]{:S(2)}) %collective-permute-start.13) | collective-permute-done | bytes 6176 | tf_op jit(solution)/shard_map/ppermute | solution.py:71
  44.0 2.9 %all-to-all-done.1.refs_4_ = bf16[32,2,768]{2,1,0:T(2,128)(2,1)S(1)} async-done(((bf16[32,2,768]{2,1,0:T(2,128)(2,1)}), bf16[32,2,768]{2,1,0:T(2,128)(2,1)S(1)}, u32[]{:S(2)}, u32[]{:S(2)}) %all-to-all-start.1) | async-done | bytes 98336 | tf_op jit(solution)/shard_map/all_to_all | solution.py:646
  46.9 0.8 %finish.1 = bf16[3,1536]{1,0:T(4,128)(2,1)} custom-call(bf16[2,1536]{1,0:T(2,128)(2,1)S(1)} %get-tuple-element.49.refs_0_, bf16[2,1536]{1,0:T(2,128)(2,1)S(1)} %collective-permute-done.11.refs_1_, bf16[2,1536]{1,0:T(2,128)(2,1)S(1)} %collective-permute-done.12.refs_2_, bf16[2,1536]{1,0:T(2,128)(2,1)S(1)} %collective-permute-done.13.refs_3_, ...), custom_call_target="tpu_custom_call" | custom-call | tf_op jit(solution)/shard_map/finish/pallas_call | solution.py:648
  (4 shorter events, 0.0 us)
Async XLA Ops:
  2.9 15.3 %all-to-all-start = ((bf16[32,2,896]{2,1,0:T(2,128)(2,1)}), bf16[32,2,896]{2,1,0:T(2,128)(2,1)S(1)}, u32[]{:S(2)}, u32[]{:S(2)}) async-start(bf16[32,2,896]{2,1,0:T(2,128)(2,1)} %get-tuple-element.31), calls=%async_computation | async-start | bytes 229376 | tf_op jit(solution)/shard_map/all_to_all | solution.py:572
  10.2 4.2 %collective-permute-start.2 = (bf16[2,1664]{1,0:T(2,128)(2,1)S(1)}, bf16[2,1664]{1,0:T(2,128)(2,1)S(1)}, u32[]{:S(2)}, u32[]{:S(2)}) collective-permute-start(bf16[2,1664]{1,0:T(2,128)(2,1)S(1)} %get-tuple-element.30.refs_0_), channel_id=1, source_target_pairs={{0,3},{1,2},{2,1},{3,0},{4,7},{5,6},{6,5},{7,4},{8,11},{9,10},{10,... | collective-permute-start | bytes 19976 | tf_op jit(solution)/shard_map/ppermute | solution.py:71
  11.8 3.7 %collective-permute-start.1 = (bf16[2,1664]{1,0:T(2,128)(2,1)S(1)}, bf16[2,1664]{1,0:T(2,128)(2,1)S(1)}, u32[]{:S(2)}, u32[]{:S(2)}) collective-permute-start(bf16[2,1664]{1,0:T(2,128)(2,1)S(1)} %get-tuple-element.30.refs_0_), channel_id=1, source_target_pairs={{0,2},{1,3},{2,0},{3,1},{4,6},{5,7},{6,4},{7,5},{8,10},{9,11},{10,... | collective-permute-start | bytes 19976 | tf_op jit(solution)/shard_map/ppermute | solution.py:71
  12.1 3.3 %collective-permute-start = (bf16[2,1664]{1,0:T(2,128)(2,1)S(1)}, bf16[2,1664]{1,0:T(2,128)(2,1)S(1)}, u32[]{:S(2)}, u32[]{:S(2)}) collective-permute-start(bf16[2,1664]{1,0:T(2,128)(2,1)S(1)} %get-tuple-element.30.refs_0_), channel_id=1, source_target_pairs={{0,1},{1,0},{2,3},{3,2},{4,5},{5,4},{6,7},{7,6},{8,9},{9,8},{10,11... | collective-permute-start | bytes 19976 | tf_op jit(solution)/shard_map/ppermute | solution.py:71
  14.4 4.7 %copy-start.1 = (bf16[384,1536]{1,0:T(8,128)(2,1)S(1)}, bf16[384,1536]{1,0:T(8,128)(2,1)}, u32[]{:S(2)}) copy-start(bf16[384,1536]{1,0:T(8,128)(2,1)} %refs_4_.3) | copy-start | bytes 3538948
  19.0 9.8 %collective-permute-start.9 = (bf16[384,1536]{1,0:T(8,128)(2,1)S(1)}, bf16[384,1536]{1,0:T(8,128)(2,1)S(1)}, u32[]{:S(2)}, u32[]{:S(2)}) collective-permute-start(bf16[384,1536]{1,0:T(8,128)(2,1)S(1)} %copy-done.1), channel_id=1, source_target_pairs={{0,1},{1,0},{2,3},{3,2},{4,5},{5,4},{6,7},{7,6},{8,9},{9,8},{10,11... | collective-permute-start | bytes 3538952 | tf_op jit(solution)/shard_map/ppermute | solution.py:598
  19.3 3.8 %collective-permute-start.3 = (bf16[6,640]{1,0:T(8,128)(2,1)S(1)}, bf16[6,640]{1,0:T(8,128)(2,1)S(1)}, u32[]{:S(2)}, u32[]{:S(2)}) collective-permute-start(bf16[6,640]{1,0:T(8,128)(2,1)S(1)} %get-tuple-element.34), channel_id=1, source_target_pairs={{0,1},{1,0},{2,3},{3,2},{4,5},{5,4},{6,7},{7,6},{8,9},{9,8},{10,11... | collective-permute-start | bytes 23048 | tf_op jit(solution)/shard_map/ppermute | solution.py:71
  19.6 3.7 %collective-permute-start.4 = (bf16[6,640]{1,0:T(8,128)(2,1)S(1)}, bf16[6,640]{1,0:T(8,128)(2,1)S(1)}, u32[]{:S(2)}, u32[]{:S(2)}) collective-permute-start(bf16[6,640]{1,0:T(8,128)(2,1)S(1)} %get-tuple-element.35), channel_id=1, source_target_pairs={{0,2},{1,3},{2,0},{3,1},{4,6},{5,7},{6,4},{7,5},{8,10},{9,11},{10,... | collective-permute-start | bytes 23048 | tf_op jit(solution)/shard_map/ppermute | solution.py:71
  20.0 3.3 %copy-start = (bf16[6,2,128,512]{3,2,1,0:T(8,128)(2,1)S(1)}, bf16[6,2,128,512]{3,2,1,0:T(8,128)(2,1)}, u32[]{:S(2)}) copy-start(bf16[6,2,128,512]{3,2,1,0:T(8,128)(2,1)} %refs_4_.2) | copy-start | bytes 4718596
  20.0 3.3 %collective-permute-start.5 = (bf16[6,640]{1,0:T(8,128)(2,1)S(1)}, bf16[6,640]{1,0:T(8,128)(2,1)S(1)}, u32[]{:S(2)}, u32[]{:S(2)}) collective-permute-start(bf16[6,640]{1,0:T(8,128)(2,1)S(1)} %get-tuple-element.36), channel_id=1, source_target_pairs={{0,3},{1,2},{2,1},{3,0},{4,7},{5,6},{6,5},{7,4},{8,11},{9,10},{10,... | collective-permute-start | bytes 23048 | tf_op jit(solution)/shard_map/ppermute | solution.py:71
  24.0 3.8 %collective-permute-start.6 = (bf16[6,896]{1,0:T(8,128)(2,1)S(1)}, bf16[6,896]{1,0:T(8,128)(2,1)S(1)}, u32[]{:S(2)}, u32[]{:S(2)}) collective-permute-start(bf16[6,896]{1,0:T(8,128)(2,1)S(1)} %get-tuple-element.40), channel_id=1, source_target_pairs={{0,1},{1,0},{2,3},{3,2},{4,5},{5,4},{6,7},{7,6},{8,9},{9,8},{10,11... | collective-permute-start | bytes 32264 | tf_op jit(solution)/shard_map/ppermute | solution.py:71
  24.5 3.7 %collective-permute-start.7 = (bf16[6,896]{1,0:T(8,128)(2,1)S(1)}, bf16[6,896]{1,0:T(8,128)(2,1)S(1)}, u32[]{:S(2)}, u32[]{:S(2)}) collective-permute-start(bf16[6,896]{1,0:T(8,128)(2,1)S(1)} %get-tuple-element.41), channel_id=1, source_target_pairs={{0,2},{1,3},{2,0},{3,1},{4,6},{5,7},{6,4},{7,5},{8,10},{9,11},{10,... | collective-permute-start | bytes 32264 | tf_op jit(solution)/shard_map/ppermute | solution.py:71
  25.7 3.1 %collective-permute-start.8 = (bf16[6,896]{1,0:T(8,128)(2,1)S(1)}, bf16[6,896]{1,0:T(8,128)(2,1)S(1)}, u32[]{:S(2)}, u32[]{:S(2)}) collective-permute-start(bf16[6,896]{1,0:T(8,128)(2,1)S(1)} %get-tuple-element.42), channel_id=1, source_target_pairs={{0,3},{1,2},{2,1},{3,0},{4,7},{5,6},{6,5},{7,4},{8,11},{9,10},{10,... | collective-permute-start | bytes 32264 | tf_op jit(solution)/shard_map/ppermute | solution.py:71
  28.9 1.8 %copy-start.3 = (f32[1536]{0:T(1024)S(1)}, f32[1536]{0:T(1024)}, u32[]{:S(2)}) copy-start(f32[1536]{0:T(1024)} %param.19) | copy-start | bytes 18436
  29.7 4.1 %collective-permute-start.10 = (bf16[12,1536]{1,0:T(8,128)(2,1)S(1)}, bf16[12,1536]{1,0:T(8,128)(2,1)S(1)}, u32[]{:S(2)}, u32[]{:S(2)}) collective-permute-start(bf16[12,1536]{1,0:T(8,128)(2,1)S(1)} %out.1.refs_0_), channel_id=1, source_target_pairs={{0,2},{1,3},{2,0},{3,1},{4,6},{5,7},{6,4},{7,5},{8,10},{9,11},{10,... | collective-permute-start | bytes 110600 | tf_op jit(solution)/shard_map/ppermute | solution.py:98
  30.7 3.1 %copy-start.2 = (bf16[1536,8]{0,1:T(8,128)(2,1)S(1)}, bf16[1536,8]{0,1:T(8,128)(2,1)}, u32[]{:S(2)}) copy-start(bf16[1536,8]{0,1:T(8,128)(2,1)} %param.20) | copy-start | bytes 73732
  36.5 10.4 %all-to-all-start.1 = ((bf16[32,2,768]{2,1,0:T(2,128)(2,1)}), bf16[32,2,768]{2,1,0:T(2,128)(2,1)S(1)}, u32[]{:S(2)}, u32[]{:S(2)}) async-start(bf16[32,2,768]{2,1,0:T(2,128)(2,1)} %get-tuple-element.53), calls=%async_computation.1 | async-start | bytes 196608 | tf_op jit(solution)/shard_map/all_to_all | solution.py:646
  39.0 2.0 %collective-permute-start.11 = (bf16[2,1536]{1,0:T(2,128)(2,1)S(1)}, bf16[2,1536]{1,0:T(2,128)(2,1)S(1)}, u32[]{:S(2)}, u32[]{:S(2)}) collective-permute-start(bf16[2,1536]{1,0:T(2,128)(2,1)S(1)} %get-tuple-element.50), channel_id=1, source_target_pairs={{0,1},{1,0},{2,3},{3,2},{4,5},{5,4},{6,7},{7,6},{8,9},{9,8},{10,11... | collective-permute-start | bytes 18440 | tf_op jit(solution)/shard_map/ppermute | solution.py:71
  39.2 3.6 %collective-permute-start.12 = (bf16[2,1536]{1,0:T(2,128)(2,1)S(1)}, bf16[2,1536]{1,0:T(2,128)(2,1)S(1)}, u32[]{:S(2)}, u32[]{:S(2)}) collective-permute-start(bf16[2,1536]{1,0:T(2,128)(2,1)S(1)} %get-tuple-element.51), channel_id=1, source_target_pairs={{0,2},{1,3},{2,0},{3,1},{4,6},{5,7},{6,4},{7,5},{8,10},{9,11},{10,... | collective-permute-start | bytes 18440 | tf_op jit(solution)/shard_map/ppermute | solution.py:71
  40.9 3.1 %collective-permute-start.13 = (bf16[2,1536]{1,0:T(2,128)(2,1)S(1)}, bf16[2,1536]{1,0:T(2,128)(2,1)S(1)}, u32[]{:S(2)}, u32[]{:S(2)}) collective-permute-start(bf16[2,1536]{1,0:T(2,128)(2,1)S(1)} %get-tuple-element.52), channel_id=1, source_target_pairs={{0,3},{1,2},{2,1},{3,0},{4,7},{5,6},{6,5},{7,4},{8,11},{9,10},{10,... | collective-permute-start | bytes 18440 | tf_op jit(solution)/shard_map/ppermute | solution.py:71

commit v3 on v2

--- a/solution.py
+++ b/solution.py
@@ -97,6 +97,13 @@
         pairs = [(me, (me + chips * CORES) % size) for me in range(size)]
         arrived.append(lax.ppermute(block, "tensor", pairs))
     return arrived
+
+
+def to_everyone(blocks):
+    order = tuple(reversed(range(blocks.shape[0])))
+    return lax.all_to_all(
+        blocks, ("replica", "tensor"), 0, 0, axis_index_groups=[order], tiled=True
+    )
 
 
 def page_hits(plan, pages):
@@ -230,7 +237,8 @@
     picked = jnp.sum(picked.reshape(-1, size, 2, half), axis=0)
     for owner in range(size):
         rows_ref[owner * home_dev : (owner + 1) * home_dev] = gathered[owner]
-        guest = jnp.concatenate([picked[owner, :1], picked[owner, 1:]], axis=1)
+        place = size - 1 - owner
+        guest = jnp.concatenate([picked[place, :1], picked[place, 1:]], axis=1)
         rows_ref[homes + owner : homes + owner + 1] = guest[:, : width + LANES]
     norm = to_step(normed(rows_ref[:, :width], gain[...]))
     products = jnp.dot(norm, weight[...], preferred_element_type=jnp.float32)
@@ -481,7 +489,7 @@
         guest = ends_ref[owner : owner + 1]
         block = jnp.concatenate([guest[:, :half], guest[:, half:]], axis=0).astype(jnp.bfloat16)
         for place in range(owner, guests.shape[0], size):
-            guests[place] = block
+            guests[guests.shape[0] - 1 - place] = block
 
 
 def finish_kernel(size, spot, *refs):
@@ -491,7 +499,8 @@
     came = guests[...].astype(jnp.float32)
     lane = lax.broadcasted_iota(jnp.int32, (1, LANES), 1)
     source = at_lane(tail[...], lane, spot).reshape(1, 1, 1)
-    place = lax.broadcasted_iota(jnp.int32, (came.shape[0], 1, 1), 0) // size
+    place = lax.broadcasted_iota(jnp.int32, (came.shape[0], 1, 1), 0)
+    place = (came.shape[0] - 1 - place) // size
     guest = jnp.sum(jnp.where(place.astype(jnp.float32) == source, came, 0.0), axis=0)
     guest = jnp.concatenate([guest[:1], guest[1:]], axis=1)
     out[...] = jnp.concatenate([homes, guest], axis=0).astype(jnp.bfloat16)
@@ -569,7 +578,7 @@
         compiler_params=PARAMS,
         name="offer",
     )(far(tokens), far(routes.T), far(guest_pages), far(page_table.T), far(home_len), packed)
-    came = lax.all_to_all(offers, ("replica", "tensor"), 0, 0, tiled=True)
+    came = to_everyone(offers)
     messages = exchanged([homes] * size)
     (qkv_near,) = loaded(homes, (qkv_weight, 0, width))
 
@@ -643,7 +652,7 @@
         router.T,
         *[resident(piece) for piece in gate_up + down],
     )
-    guests = lax.all_to_all(guests, ("replica", "tensor"), 0, 0, tiled=True)
+    guests = to_everyone(guests)
     pieces = exchanged(pieces)
     return pl.pallas_call(
         functools.partial(finish_kernel, size, top + 1 + MAXP),

time: 48 us -> 47.7 us (level)
  waiting for transfers between devices: 12.1 us -> 11.6 us
where the time goes in v3:
time: 47.7 us; the launch traced here: 47.3 us
  starting transfers between devices  18.8 us (39%)
  Pallas kernels  14.7 us (31%)
  waiting for transfers between devices  11.6 us (24%)
  between operations  1.43 us (3%)
  local copies, waits for them, and re-layouts  0.73 us (2%)
    all_to_all x2, starting transfers between devices, to_everyone(): lax.all_to_all(blocks, ('replica', 'tensor'), 0, 0, axis_index_groups=[or...  9.88 us
    ppermute x12, starting transfers between devices, exchanged(): arrived.append(lax.ppermute(block, 'tensor', pairs))  7.83 us
    pallas_call x4, Pallas kernels, loaded(): pl.pallas_call(functools.partial(load_kernel, tuple(plans)), out_shape=sh...  7.31 us
    ppermute x12, waiting for transfers between devices, exchanged(): arrived.append(lax.ppermute(block, 'tensor', pairs))  5.35 us
    all_to_all x2, waiting for transfers between devices, to_everyone(): lax.all_to_all(blocks, ('replica', 'tensor'), 0, 0, axis_index_groups=[or...  5.18 us
    pallas_call x1, Pallas kernels, shards(): pl.pallas_call(functools.partial(expert_kernel, size, top, router.shape[1...  2.64 us
    pallas_call x1, Pallas kernels, shards(): pl.pallas_call(offer_kernel, out_shape=[shape((everyone, 2, (wide + LANES...  1.58 us
    ppermute x1, waiting for transfers between devices, across(): arrived.append(lax.ppermute(block, 'tensor', pairs))  1.09 us
  transfers between devices with their start and end apart: 16, of which 9 were waited for; matrix products, arithmetic and copies ran while one was open for 1% of the time, Pallas kernels for 17%

profile of v3, /device:TPU:0, one launch (start us, length us, event | category | flops | bytes accessed | tf_op | source)
XLA Modules:
  0.0 47.3 jit_solution(10238653233780148932)
XLA Ops:
  1.3 1.6 %offer.1 = (bf16[32,2,896]{2,1,0:T(2,128)(2,1)}, bf16[2,1664]{1,0:T(2,128)(2,1)S(1)}, f32[6,128]{1,0:T(8,128)S(1)}, f32[1,128]{1,0:T(1,128)S(1)}) custom-call(bf16[3,1536]{1,0:T(4,128)(2,1)} %tokens.1, s32[6,12]{1,0:T(8,128)} %bitcast.12, s32[1,2]{1,0:T(1,128)} %pages.1, s32[2,8]{1,0:T(2,128)} %bitcast.13, s32[8]{0:T(128)} %lens.1, s32[1]{0:T(128)S(6)} %add.3.packed), custom_call_target="tpu_custom_call" | custom-call | tf_op jit(solution)/shard_map/offer/pallas_call | solution.py:560
  2.9 7.3 %all-to-all-start = ((bf16[32,2,896]{2,1,0:T(2,128)(2,1)}), bf16[32,2,896]{2,1,0:T(2,128)(2,1)S(1)}, u32[]{:S(2)}, u32[]{:S(2)}) async-start(bf16[32,2,896]{2,1,0:T(2,128)(2,1)} %get-tuple-element.31), calls=%async_computation | async-start | bytes 229376 | tf_op jit(solution)/shard_map/all_to_all | solution.py:104
  10.2 1.6 %collective-permute-start.2 = (bf16[2,1664]{1,0:T(2,128)(2,1)S(1)}, bf16[2,1664]{1,0:T(2,128)(2,1)S(1)}, u32[]{:S(2)}, u32[]{:S(2)}) collective-permute-start(bf16[2,1664]{1,0:T(2,128)(2,1)S(1)} %get-tuple-element.30.refs_0_), channel_id=1, source_target_pairs={{0,3},{1,2},{2,1},{3,0},{4,7},{5,6},{6,5},{7,4},{8,11},{9,10},{10,... | collective-permute-start | bytes 19976 | tf_op jit(solution)/shard_map/ppermute | solution.py:71
  11.8 0.4 collective-permute-start.1
  12.1 0.0 collective-permute-start
  12.2 0.7 %reshape.15.refs_5_ = f32[1,1536]{1,0:T(1,128)S(1)} reshape(f32[1536]{0:T(1024)} %param.16) | data formatting | bytes 12288 | tf_op jit(solution)/shard_map/reshape | solution.py:599
  12.9 1.5 %load.4.refs_6_ = bf16[1536,640]{1,0:T(8,128)(2,1)S(1)} custom-call(bf16[2,1664]{1,0:T(2,128)(2,1)S(1)} %get-tuple-element.30.refs_0_, bf16[1536,640]{1,0:T(8,128)(2,1)} %refs_1_.4), custom_call_target="tpu_custom_call" | custom-call | bytes 1966080 | tf_op jit(solution)/shard_map/load/pallas_call | solution.py:202
  14.4 0.0 copy-start.1
  14.4 0.0 collective-permute-done.2.refs_3_
  14.4 1.0 %collective-permute-done.1.refs_2_ = bf16[2,1664]{1,0:T(2,128)(2,1)S(1)} collective-permute-done((bf16[2,1664]{1,0:T(2,128)(2,1)S(1)}, bf16[2,1664]{1,0:T(2,128)(2,1)S(1)}, u32[]{:S(2)}, u32[]{:S(2)}) %collective-permute-start.1) | collective-permute-done | bytes 6688 | tf_op jit(solution)/shard_map/ppermute | solution.py:71
  15.4 0.0 collective-permute-done.refs_1_
  15.4 2.5 %all-to-all-done.refs_4_ = bf16[32,2,896]{2,1,0:T(2,128)(2,1)S(1)} async-done(((bf16[32,2,896]{2,1,0:T(2,128)(2,1)}), bf16[32,2,896]{2,1,0:T(2,128)(2,1)S(1)}, u32[]{:S(2)}, u32[]{:S(2)}) %all-to-all-start) | async-done | bytes 114720 | tf_op jit(solution)/shard_map/all_to_all | solution.py:104
  18.0 0.8 %project.1 = (f32[12,1664]{1,0:T(8,128)S(1)}, bf16[6,640]{1,0:T(8,128)(2,1)S(1)}, bf16[6,640]{1,0:T(8,128)(2,1)S(1)}, bf16[6,640]{1,0:T(8,128)(2,1)S(1)}, bf16[6,640]{1,0:T(8,128)(2,1)S(1)}) custom-call(bf16[2,1664]{1,0:T(2,128)(2,1)S(1)} %get-tuple-element.30.refs_0_, bf16[2,1664]{1,0:T(2,128)(2,1)S(1)} %collective-permute-done.refs_1_, ...), custom_call_target="tpu_custom_call" | custom-call | tf_op jit(solution)/shard_map/project/pallas_call | solution.py:585
  18.8 0.0 copy-done.1
  18.8 0.1 collective-permute-start.9
  18.9 0.5 %collective-permute-start.3 = (bf16[6,640]{1,0:T(8,128)(2,1)S(1)}, bf16[6,640]{1,0:T(8,128)(2,1)S(1)}, u32[]{:S(2)}, u32[]{:S(2)}) collective-permute-start(bf16[6,640]{1,0:T(8,128)(2,1)S(1)} %get-tuple-element.34), channel_id=1, source_target_pairs={{0,1},{1,0},{2,3},{3,2},{4,5},{5,4},{6,7},{7,6},{8,9},{9,8},{10,11... | collective-permute-start | bytes 23048 | tf_op jit(solution)/shard_map/ppermute | solution.py:71
  19.4 1.0 %collective-permute-start.4 = (bf16[6,640]{1,0:T(8,128)(2,1)S(1)}, bf16[6,640]{1,0:T(8,128)(2,1)S(1)}, u32[]{:S(2)}, u32[]{:S(2)}) collective-permute-start(bf16[6,640]{1,0:T(8,128)(2,1)S(1)} %get-tuple-element.35), channel_id=1, source_target_pairs={{0,2},{1,3},{2,0},{3,1},{4,6},{5,7},{6,4},{7,5},{8,10},{9,11},{10,... | collective-permute-start | bytes 23048 | tf_op jit(solution)/shard_map/ppermute | solution.py:71
  20.4 0.4 collective-permute-start.5
  20.8 2.0 %load.5 = (bf16[2,1536,2,128]{3,2,1,0:T(2,128)(2,1)S(1)}, bf16[512,1536]{1,0:T(8,128)(2,1)S(1)}) custom-call(f32[12,1664]{1,0:T(8,128)S(1)} %get-tuple-element.37.refs_0_.refs_5_.refs_2_, bf16[1536,2,1024]{2,1,0:T(2,128)(2,1)} %refs_1_.7, bf16[1024,1536]{1,0:T(8,128)(2,1)} %refs_2_.5), custom_call_target="tpu_custom_call" | custom-call | bytes 3145728 | tf_op jit(solution)/shard_map/load/pallas_call | solution.py:202
  22.8 0.0 collective-permute-done.3.refs_1_
  22.8 0.3 collective-permute-done.4.refs_2_
  23.0 0.5 %collective-permute-done.5.refs_3_ = bf16[6,640]{1,0:T(8,128)(2,1)S(1)} collective-permute-done((bf16[6,640]{1,0:T(8,128)(2,1)S(1)}, bf16[6,640]{1,0:T(8,128)(2,1)S(1)}, u32[]{:S(2)}, u32[]{:S(2)}) %collective-permute-start.5) | collective-permute-done | bytes 7712 | tf_op jit(solution)/shard_map/ppermute | solution.py:71
  23.6 0.0 copy-done
  23.6 0.7 %attend.1 = (bf16[6,896]{1,0:T(8,128)(2,1)S(1)}, bf16[6,896]{1,0:T(8,128)(2,1)S(1)}, bf16[6,896]{1,0:T(8,128)(2,1)S(1)}, bf16[6,896]{1,0:T(8,128)(2,1)S(1)}) custom-call(bf16[6,640]{1,0:T(8,128)(2,1)S(1)} %get-tuple-element.33.refs_0_, bf16[6,640]{1,0:T(8,128)(2,1)S(1)} %collective-permute-done.3.refs_1_, bf16[6,640]{1,0:T(8,128)(2,1)S(1)} %collective-permute-done.4.refs_2_, ...), custom_call_target="tpu_custom_call" | custom-call | tf_op jit(solution)/shard_map/attend/pallas_call | solution.py:608
  24.3 0.2 collective-permute-start.6
  24.5 1.0 %collective-permute-start.7 = (bf16[6,896]{1,0:T(8,128)(2,1)S(1)}, bf16[6,896]{1,0:T(8,128)(2,1)S(1)}, u32[]{:S(2)}, u32[]{:S(2)}) collective-permute-start(bf16[6,896]{1,0:T(8,128)(2,1)S(1)} %get-tuple-element.41), channel_id=1, source_target_pairs={{0,2},{1,3},{2,0},{3,1},{4,6},{5,7},{6,4},{7,5},{8,10},{9,11},{10,... | collective-permute-start | bytes 32264 | tf_op jit(solution)/shard_map/ppermute | solution.py:71
  25.5 0.8 %collective-permute-start.8 = (bf16[6,896]{1,0:T(8,128)(2,1)S(1)}, bf16[6,896]{1,0:T(8,128)(2,1)S(1)}, u32[]{:S(2)}, u32[]{:S(2)}) collective-permute-start(bf16[6,896]{1,0:T(8,128)(2,1)S(1)} %get-tuple-element.42), channel_id=1, source_target_pairs={{0,3},{1,2},{2,1},{3,0},{4,7},{5,6},{6,5},{7,4},{8,11},{9,10},{10,... | collective-permute-start | bytes 32264 | tf_op jit(solution)/shard_map/ppermute | solution.py:71
  26.3 1.9 %load.6 = (bf16[3,1536,2,128]{3,2,1,0:T(2,128)(2,1)S(1)}, bf16[256,1536]{1,0:T(8,128)(2,1)S(1)}) custom-call(bf16[6,896]{1,0:T(8,128)(2,1)S(1)} %get-tuple-element.39.refs_0_, bf16[1536,2,1024]{2,1,0:T(2,128)(2,1)} %refs_1_.7, bf16[1024,1536]{1,0:T(8,128)(2,1)} %refs_2_.5), custom_call_target="tpu_custom_call" | custom-call | bytes 3145728 | tf_op jit(solution)/shard_map/load/pallas_call | solution.py:202
  28.2 0.0 collective-permute-done.6.refs_1_
  28.2 0.0 collective-permute-done.7.refs_2_
  28.2 0.4 collective-permute-done.8.refs_3_
  28.6 0.0 collective-permute-done.9.refs_5_
  28.6 0.8 %out.1.refs_0_ = bf16[12,1536]{1,0:T(8,128)(2,1)S(1)} custom-call(bf16[6,896]{1,0:T(8,128)(2,1)S(1)} %get-tuple-element.39.refs_0_, bf16[6,896]{1,0:T(8,128)(2,1)S(1)} %collective-permute-done.6.refs_1_, bf16[6,896]{1,0:T(8,128)(2,1)S(1)} %collective-permute-done.7.refs_2_, bf16[6,896]{1,0:T(8,128)(2,1)S(1)} %collective-permute-done.8.refs_3_, ...), custom_call_target="tpu_custom_call" | custom-call | tf_op jit(solution)/shard_map/out/pallas_call | solution.py:623
  29.5 1.0 %collective-permute-start.10 = (bf16[12,1536]{1,0:T(8,128)(2,1)S(1)}, bf16[12,1536]{1,0:T(8,128)(2,1)S(1)}, u32[]{:S(2)}, u32[]{:S(2)}) collective-permute-start(bf16[12,1536]{1,0:T(8,128)(2,1)S(1)} %out.1.refs_0_), channel_id=1, source_target_pairs={{0,2},{1,3},{2,0},{3,1},{4,6},{5,7},{6,4},{7,5},{8,10},{9,11},{10,... | collective-permute-start | bytes 110600 | tf_op jit(solution)/shard_map/ppermute | solution.py:98
  30.5 0.0 copy-done.3
  30.5 0.0 copy-start.2
  30.5 2.0 %load.7 = (bf16[3,1536,2,128]{3,2,1,0:T(2,128)(2,1)S(1)}, bf16[256,1536]{1,0:T(8,128)(2,1)S(1)}) custom-call(bf16[12,1536]{1,0:T(8,128)(2,1)S(1)} %out.1.refs_0_, bf16[1536,2,1024]{2,1,0:T(2,128)(2,1)} %refs_1_.7, bf16[1024,1536]{1,0:T(8,128)(2,1)} %refs_2_.5), custom_call_target="tpu_custom_call" | custom-call | bytes 3145728 | tf_op jit(solution)/shard_map/load/pallas_call | solution.py:202
  32.5 1.1 %collective-permute-done.10.refs_1_ = bf16[12,1536]{1,0:T(8,128)(2,1)S(1)} collective-permute-done((bf16[12,1536]{1,0:T(8,128)(2,1)S(1)}, bf16[12,1536]{1,0:T(8,128)(2,1)S(1)}, u32[]{:S(2)}, u32[]{:S(2)}) %collective-permute-start.10) | collective-permute-done | bytes 36896 | tf_op jit(solution)/shard_map/ppermute | solution.py:98
  33.6 2.6 %experts.1 = (bf16[2,1536]{1,0:T(2,128)(2,1)S(1)}, bf16[2,1536]{1,0:T(2,128)(2,1)S(1)}, bf16[2,1536]{1,0:T(2,128)(2,1)S(1)}, bf16[2,1536]{1,0:T(2,128)(2,1)S(1)}, bf16[32,2,768]{2,1,0:T(2,128)(2,1)}) custom-call(bf16[12,1536]{1,0:T(8,128)(2,1)S(1)} %out.1.refs_0_, bf16[12,1536]{1,0:T(8,128)(2,1)S(1)} %collective-permute-done.10.refs_1_, ...), custom_call_target="tpu_custom_call" | custom-call | tf_op jit(solution)/shard_map/experts/pallas_call | solution.py:634
  36.2 2.6 %all-to-all-start.1 = ((bf16[32,2,768]{2,1,0:T(2,128)(2,1)}), bf16[32,2,768]{2,1,0:T(2,128)(2,1)S(1)}, u32[]{:S(2)}, u32[]{:S(2)}) async-start(bf16[32,2,768]{2,1,0:T(2,128)(2,1)} %get-tuple-element.53), calls=%async_computation.1 | async-start | bytes 196608 | tf_op jit(solution)/shard_map/all_to_all | solution.py:104
  38.8 0.3 collective-permute-start.11
  39.1 1.7 %collective-permute-start.12 = (bf16[2,1536]{1,0:T(2,128)(2,1)S(1)}, bf16[2,1536]{1,0:T(2,128)(2,1)S(1)}, u32[]{:S(2)}, u32[]{:S(2)}) collective-permute-start(bf16[2,1536]{1,0:T(2,128)(2,1)S(1)} %get-tuple-element.51), channel_id=1, source_target_pairs={{0,2},{1,3},{2,0},{3,1},{4,6},{5,7},{6,4},{7,5},{8,10},{9,11},{10,... | collective-permute-start | bytes 18440 | tf_op jit(solution)/shard_map/ppermute | solution.py:71
  40.8 0.0 collective-permute-start.13
  40.8 0.0 collective-permute-done.11.refs_1_
  40.8 1.9 %collective-permute-done.12.refs_2_ = bf16[2,1536]{1,0:T(2,128)(2,1)S(1)} collective-permute-done((bf16[2,1536]{1,0:T(2,128)(2,1)S(1)}, bf16[2,1536]{1,0:T(2,128)(2,1)S(1)}, u32[]{:S(2)}, u32[]{:S(2)}) %collective-permute-start.12) | collective-permute-done | bytes 6176 | tf_op jit(solution)/shard_map/ppermute | solution.py:71
  42.8 1.1 %collective-permute-done.13.refs_3_ = bf16[2,1536]{1,0:T(2,128)(2,1)S(1)} collective-permute-done((bf16[2,1536]{1,0:T(2,128)(2,1)S(1)}, bf16[2,1536]{1,0:T(2,128)(2,1)S(1)}, u32[]{:S(2)}, u32[]{:S(2)}) %collective-permute-start.13) | collective-permute-done | bytes 6176 | tf_op jit(solution)/shard_map/ppermute | solution.py:71
  43.9 2.6 %all-to-all-done.1.refs_4_ = bf16[32,2,768]{2,1,0:T(2,128)(2,1)S(1)} async-done(((bf16[32,2,768]{2,1,0:T(2,128)(2,1)}), bf16[32,2,768]{2,1,0:T(2,128)(2,1)S(1)}, u32[]{:S(2)}, u32[]{:S(2)}) %all-to-all-start.1) | async-done | bytes 98336 | tf_op jit(solution)/shard_map/all_to_all | solution.py:104
  46.5 0.8 %finish.1 = bf16[3,1536]{1,0:T(4,128)(2,1)} custom-call(bf16[2,1536]{1,0:T(2,128)(2,1)S(1)} %get-tuple-element.49.refs_0_, bf16[2,1536]{1,0:T(2,128)(2,1)S(1)} %collective-permute-done.11.refs_1_, bf16[2,1536]{1,0:T(2,128)(2,1)S(1)} %collective-permute-done.12.refs_2_, bf16[2,1536]{1,0:T(2,128)(2,1)S(1)} %collective-permute-done.13.refs_3_, ...), custom_call_target="tpu_custom_call" | custom-call | tf_op jit(solution)/shard_map/finish/pallas_call | solution.py:657
  (4 shorter events, 0.0 us)
Async XLA Ops:
  2.9 15.1 %all-to-all-start = ((bf16[32,2,896]{2,1,0:T(2,128)(2,1)}), bf16[32,2,896]{2,1,0:T(2,128)(2,1)S(1)}, u32[]{:S(2)}, u32[]{:S(2)}) async-start(bf16[32,2,896]{2,1,0:T(2,128)(2,1)} %get-tuple-element.31), calls=%async_computation | async-start | bytes 229376 | tf_op jit(solution)/shard_map/all_to_all | solution.py:104
  10.2 4.2 %collective-permute-start.2 = (bf16[2,1664]{1,0:T(2,128)(2,1)S(1)}, bf16[2,1664]{1,0:T(2,128)(2,1)S(1)}, u32[]{:S(2)}, u32[]{:S(2)}) collective-permute-start(bf16[2,1664]{1,0:T(2,128)(2,1)S(1)} %get-tuple-element.30.refs_0_), channel_id=1, source_target_pairs={{0,3},{1,2},{2,1},{3,0},{4,7},{5,6},{6,5},{7,4},{8,11},{9,10},{10,... | collective-permute-start | bytes 19976 | tf_op jit(solution)/shard_map/ppermute | solution.py:71
  11.8 3.7 %collective-permute-start.1 = (bf16[2,1664]{1,0:T(2,128)(2,1)S(1)}, bf16[2,1664]{1,0:T(2,128)(2,1)S(1)}, u32[]{:S(2)}, u32[]{:S(2)}) collective-permute-start(bf16[2,1664]{1,0:T(2,128)(2,1)S(1)} %get-tuple-element.30.refs_0_), channel_id=1, source_target_pairs={{0,2},{1,3},{2,0},{3,1},{4,6},{5,7},{6,4},{7,5},{8,10},{9,11},{10,... | collective-permute-start | bytes 19976 | tf_op jit(solution)/shard_map/ppermute | solution.py:71
  12.1 3.3 %collective-permute-start = (bf16[2,1664]{1,0:T(2,128)(2,1)S(1)}, bf16[2,1664]{1,0:T(2,128)(2,1)S(1)}, u32[]{:S(2)}, u32[]{:S(2)}) collective-permute-start(bf16[2,1664]{1,0:T(2,128)(2,1)S(1)} %get-tuple-element.30.refs_0_), channel_id=1, source_target_pairs={{0,1},{1,0},{2,3},{3,2},{4,5},{5,4},{6,7},{7,6},{8,9},{9,8},{10,11... | collective-permute-start | bytes 19976 | tf_op jit(solution)/shard_map/ppermute | solution.py:71
  14.4 4.4 %copy-start.1 = (bf16[384,1536]{1,0:T(8,128)(2,1)S(1)}, bf16[384,1536]{1,0:T(8,128)(2,1)}, u32[]{:S(2)}) copy-start(bf16[384,1536]{1,0:T(8,128)(2,1)} %refs_4_.3) | copy-start | bytes 3538948
  18.8 9.8 %collective-permute-start.9 = (bf16[384,1536]{1,0:T(8,128)(2,1)S(1)}, bf16[384,1536]{1,0:T(8,128)(2,1)S(1)}, u32[]{:S(2)}, u32[]{:S(2)}) collective-permute-start(bf16[384,1536]{1,0:T(8,128)(2,1)S(1)} %copy-done.1), channel_id=1, source_target_pairs={{0,1},{1,0},{2,3},{3,2},{4,5},{5,4},{6,7},{7,6},{8,9},{9,8},{10,11... | collective-permute-start | bytes 3538952 | tf_op jit(solution)/shard_map/ppermute | solution.py:607
  18.9 3.9 %collective-permute-start.3 = (bf16[6,640]{1,0:T(8,128)(2,1)S(1)}, bf16[6,640]{1,0:T(8,128)(2,1)S(1)}, u32[]{:S(2)}, u32[]{:S(2)}) collective-permute-start(bf16[6,640]{1,0:T(8,128)(2,1)S(1)} %get-tuple-element.34), channel_id=1, source_target_pairs={{0,1},{1,0},{2,3},{3,2},{4,5},{5,4},{6,7},{7,6},{8,9},{9,8},{10,11... | collective-permute-start | bytes 23048 | tf_op jit(solution)/shard_map/ppermute | solution.py:71
  19.4 3.7 %collective-permute-start.4 = (bf16[6,640]{1,0:T(8,128)(2,1)S(1)}, bf16[6,640]{1,0:T(8,128)(2,1)S(1)}, u32[]{:S(2)}, u32[]{:S(2)}) collective-permute-start(bf16[6,640]{1,0:T(8,128)(2,1)S(1)} %get-tuple-element.35), channel_id=1, source_target_pairs={{0,2},{1,3},{2,0},{3,1},{4,6},{5,7},{6,4},{7,5},{8,10},{9,11},{10,... | collective-permute-start | bytes 23048 | tf_op jit(solution)/shard_map/ppermute | solution.py:71
  20.4 3.2 %copy-start = (bf16[6,2,128,512]{3,2,1,0:T(8,128)(2,1)S(1)}, bf16[6,2,128,512]{3,2,1,0:T(8,128)(2,1)}, u32[]{:S(2)}) copy-start(bf16[6,2,128,512]{3,2,1,0:T(8,128)(2,1)} %refs_4_.2) | copy-start | bytes 4718596
  20.4 3.2 %collective-permute-start.5 = (bf16[6,640]{1,0:T(8,128)(2,1)S(1)}, bf16[6,640]{1,0:T(8,128)(2,1)S(1)}, u32[]{:S(2)}, u32[]{:S(2)}) collective-permute-start(bf16[6,640]{1,0:T(8,128)(2,1)S(1)} %get-tuple-element.36), channel_id=1, source_target_pairs={{0,3},{1,2},{2,1},{3,0},{4,7},{5,6},{6,5},{7,4},{8,11},{9,10},{10,... | collective-permute-start | bytes 23048 | tf_op jit(solution)/shard_map/ppermute | solution.py:71
  24.3 3.9 %collective-permute-start.6 = (bf16[6,896]{1,0:T(8,128)(2,1)S(1)}, bf16[6,896]{1,0:T(8,128)(2,1)S(1)}, u32[]{:S(2)}, u32[]{:S(2)}) collective-permute-start(bf16[6,896]{1,0:T(8,128)(2,1)S(1)} %get-tuple-element.40), channel_id=1, source_target_pairs={{0,1},{1,0},{2,3},{3,2},{4,5},{5,4},{6,7},{7,6},{8,9},{9,8},{10,11... | collective-permute-start | bytes 32264 | tf_op jit(solution)/shard_map/ppermute | solution.py:71
  24.5 3.7 %collective-permute-start.7 = (bf16[6,896]{1,0:T(8,128)(2,1)S(1)}, bf16[6,896]{1,0:T(8,128)(2,1)S(1)}, u32[]{:S(2)}, u32[]{:S(2)}) collective-permute-start(bf16[6,896]{1,0:T(8,128)(2,1)S(1)} %get-tuple-element.41), channel_id=1, source_target_pairs={{0,2},{1,3},{2,0},{3,1},{4,6},{5,7},{6,4},{7,5},{8,10},{9,11},{10,... | collective-permute-start | bytes 32264 | tf_op jit(solution)/shard_map/ppermute | solution.py:71
  25.5 3.1 %collective-permute-start.8 = (bf16[6,896]{1,0:T(8,128)(2,1)S(1)}, bf16[6,896]{1,0:T(8,128)(2,1)S(1)}, u32[]{:S(2)}, u32[]{:S(2)}) collective-permute-start(bf16[6,896]{1,0:T(8,128)(2,1)S(1)} %get-tuple-element.42), channel_id=1, source_target_pairs={{0,3},{1,2},{2,1},{3,0},{4,7},{5,6},{6,5},{7,4},{8,11},{9,10},{10,... | collective-permute-start | bytes 32264 | tf_op jit(solution)/shard_map/ppermute | solution.py:71
  28.6 1.9 %copy-start.3 = (f32[1536]{0:T(1024)S(1)}, f32[1536]{0:T(1024)}, u32[]{:S(2)}) copy-start(f32[1536]{0:T(1024)} %param.19) | copy-start | bytes 18436
  29.5 4.1 %collective-permute-start.10 = (bf16[12,1536]{1,0:T(8,128)(2,1)S(1)}, bf16[12,1536]{1,0:T(8,128)(2,1)S(1)}, u32[]{:S(2)}, u32[]{:S(2)}) collective-permute-start(bf16[12,1536]{1,0:T(8,128)(2,1)S(1)} %out.1.refs_0_), channel_id=1, source_target_pairs={{0,2},{1,3},{2,0},{3,1},{4,6},{5,7},{6,4},{7,5},{8,10},{9,11},{10,... | collective-permute-start | bytes 110600 | tf_op jit(solution)/shard_map/ppermute | solution.py:98
  30.5 3.1 %copy-start.2 = (bf16[1536,8]{0,1:T(8,128)(2,1)S(1)}, bf16[1536,8]{0,1:T(8,128)(2,1)}, u32[]{:S(2)}) copy-start(bf16[1536,8]{0,1:T(8,128)(2,1)} %param.20) | copy-start | bytes 73732
  36.2 10.3 %all-to-all-start.1 = ((bf16[32,2,768]{2,1,0:T(2,128)(2,1)}), bf16[32,2,768]{2,1,0:T(2,128)(2,1)S(1)}, u32[]{:S(2)}, u32[]{:S(2)}) async-start(bf16[32,2,768]{2,1,0:T(2,128)(2,1)} %get-tuple-element.53), calls=%async_computation.1 | async-start | bytes 196608 | tf_op jit(solution)/shard_map/all_to_all | solution.py:104
  38.8 2.0 %collective-permute-start.11 = (bf16[2,1536]{1,0:T(2,128)(2,1)S(1)}, bf16[2,1536]{1,0:T(2,128)(2,1)S(1)}, u32[]{:S(2)}, u32[]{:S(2)}) collective-permute-start(bf16[2,1536]{1,0:T(2,128)(2,1)S(1)} %get-tuple-element.50), channel_id=1, source_target_pairs={{0,1},{1,0},{2,3},{3,2},{4,5},{5,4},{6,7},{7,6},{8,9},{9,8},{10,11... | collective-permute-start | bytes 18440 | tf_op jit(solution)/shard_map/ppermute | solution.py:71
  39.1 3.6 %collective-permute-start.12 = (bf16[2,1536]{1,0:T(2,128)(2,1)S(1)}, bf16[2,1536]{1,0:T(2,128)(2,1)S(1)}, u32[]{:S(2)}, u32[]{:S(2)}) collective-permute-start(bf16[2,1536]{1,0:T(2,128)(2,1)S(1)} %get-tuple-element.51), channel_id=1, source_target_pairs={{0,2},{1,3},{2,0},{3,1},{4,6},{5,7},{6,4},{7,5},{8,10},{9,11},{10,... | collective-permute-start | bytes 18440 | tf_op jit(solution)/shard_map/ppermute | solution.py:71
  40.8 3.1 %collective-permute-start.13 = (bf16[2,1536]{1,0:T(2,128)(2,1)S(1)}, bf16[2,1536]{1,0:T(2,128)(2,1)S(1)}, u32[]{:S(2)}, u32[]{:S(2)}) collective-permute-start(bf16[2,1536]{1,0:T(2,128)(2,1)S(1)} %get-tuple-element.52), channel_id=1, source_target_pairs={{0,3},{1,2},{2,1},{3,0},{4,7},{5,6},{6,5},{7,4},{8,11},{9,10},{10,... | collective-permute-start | bytes 18440 | tf_op jit(solution)/shard_map/ppermute | solution.py:71
